TPU v7x, 512 devices: a whole 4x4x16 slice. The times are simulated.
512 devices in a mesh: patch: 64 (over x, y, z_lo), band: 8 (over z_hi, core).
Axes of the slice: x: 4, y: 4, z: 16 (z_hi: 4, z_lo: 4; z = z_hi * 4 + z_lo), core: 2. Of those that a mesh axis runs over, the one named last changes fastest.
Arguments:
- pixels: bfloat16 [16384, 16, 256], P('patch', 'band'), may hold values from -6 to 6
- cotangent: bfloat16 [16384, 1024], P('patch', 'band'), may hold values from -0.03125 to 0.03125
- avail: int32 [16, 16], P(None, 'band'), may hold values 0 or 1
- band_index: int32 [16], P('band'), may hold values from 0 to 207
- band_sensor: int32 [16], P('band'), may hold values from 0 to 3
- wave_table: float32 [208], replicated, may hold values from 0.4 to 12
- first_weight: float32 [128, 128], replicated, may hold values from -0.5 to 0.5
- sensor_embed: float32 [4, 128], replicated, may hold values from -6 to 6
- out_weight: bfloat16 [128, 1024, 256], P(None, 'patch'), may hold values from -0.0078125 to 0.0078125
Outputs:
- embed: bfloat16 [16384, 1024], P('patch', 'band')
- grad_out: float32 [128, 1024, 256], P(None, 'patch')
- grad_first: float32 [128, 128], replicated
- grad_sensor: float32 [4, 128], replicated
All inputs are finite; a program needn't handle non-finite values. No bound on the sum of `avail` on one device may be relied on, other than what follows from the above.
Results may differ from a plain program's by a relative error of at most 0.017.
Values may be sent and summed in bfloat16 or wider, within the bound.
No kernel may reach another device: no remote copies, remote signals or barrier semaphores. Data moves between devices by JAX's collectives and lax.ppermute only.
A program may use at most 64 MiB of HBM per device.

v0:
```python
import math

import jax
import jax.numpy as jnp
from jax import lax
from jax.sharding import PartitionSpec as P

TILE_PATCHES = 1024


def wave_features(waves, width):
    half = width // 2
    steps = jnp.arange(half, dtype=jnp.float32)
    freqs = jnp.exp(steps * (math.log(100.0) / half))
    angles = waves[:, None] * freqs[None, :]
    return jnp.concatenate([jnp.sin(angles), jnp.cos(angles)], axis=1)


def silu_slope(preact):
    sigma = jax.nn.sigmoid(preact)
    return sigma * (1.0 + preact * (1.0 - sigma))


def hypernet(band_index, band_sensor, wave_table, first_weight, sensor_embed):
    highest = lax.Precision.HIGHEST
    table_hot = (
        band_index[:, None] == jnp.arange(wave_table.shape[0], dtype=jnp.int32)[None, :]
    ).astype(jnp.float32)
    waves = jnp.dot(table_hot, wave_table, precision=highest)
    features = wave_features(waves, first_weight.shape[0])
    sensor_hot = (
        band_sensor[:, None] == jnp.arange(sensor_embed.shape[0], dtype=jnp.int32)[None, :]
    ).astype(jnp.float32)
    preact = jnp.dot(features, first_weight, precision=highest) + jnp.dot(
        sensor_hot, sensor_embed, precision=highest
    )
    return (features, sensor_hot, preact)


def local(
    pixels,
    cotangent,
    avail,
    band_index,
    band_sensor,
    wave_table,
    first_weight,
    sensor_embed,
    out_weight,
):
    highest = lax.Precision.HIGHEST
    patch_rows = pixels.shape[0]
    row_index = lax.axis_index("patch") * patch_rows + jnp.arange(patch_rows, dtype=jnp.int32)
    tile_index = row_index // TILE_PATCHES
    tile_hot = (tile_index[:, None] == jnp.arange(avail.shape[0], dtype=jnp.int32)[None, :]).astype(
        jnp.float32
    )
    row_mask = jnp.dot(tile_hot, avail.astype(jnp.float32)).astype(jnp.bfloat16)
    masked = pixels * row_mask[:, :, None]
    features, sensor_hot, preact = hypernet(
        band_index, band_sensor, wave_table, first_weight, sensor_embed
    )
    hidden = jax.nn.silu(preact).astype(jnp.bfloat16)
    kernel_part = jnp.einsum(
        "ch,hdp->cdp", hidden, out_weight, preferred_element_type=jnp.float32
    ).astype(jnp.bfloat16)
    partial_embed = jnp.einsum(
        "tcp,cdp->td",
        masked,
        lax.all_gather(kernel_part, "patch", axis=1, tiled=True),
        preferred_element_type=jnp.float32,
    )
    rounded = lax.optimization_barrier(partial_embed.astype(jnp.bfloat16)).astype(jnp.float32)
    embed = lax.psum_scatter(rounded.astype(jnp.bfloat16), "band", scatter_dimension=1, tiled=True)
    full_cot = lax.all_gather(cotangent, "band", axis=1, tiled=True)
    kernel_grad = lax.psum_scatter(
        jnp.einsum("td,tcp->dcp", full_cot, masked, preferred_element_type=jnp.float32),
        "patch",
        scatter_dimension=0,
        tiled=True,
    )
    wide_weight = out_weight.astype(jnp.float32)
    part_out = jnp.einsum("ch,dcp->hdp", hidden.astype(jnp.float32), kernel_grad, precision=highest)
    grad_out = lax.psum(part_out, "band")
    part_hidden = jnp.einsum("dcp,hdp->ch", kernel_grad, wide_weight, precision=highest)
    grad_hidden = lax.psum(part_hidden, "patch")
    grad_pre = grad_hidden * silu_slope(preact)
    first_part = jnp.dot(features.T, grad_pre, precision=highest)
    sensor_part = jnp.dot(sensor_hot.T, grad_pre, precision=highest)
    grad_first, grad_sensor = lax.psum((first_part, sensor_part), "band")
    return (embed, grad_out, grad_first, grad_sensor)


def solution(mesh):
    placed = (
        P("patch", "band", None),
        P("patch", "band"),
        P(None, "band"),
        P("band"),
        P("band"),
        P(),
        P(),
        P(),
        P(None, "patch", None),
    )
    return jax.shard_map(
        local,
        mesh=mesh,
        in_specs=placed,
        out_specs=(P("patch", "band"), P(None, "patch", None), P(), P()),
        check_vma=False,
    )
```

profile of v0, /device:TPU:1, one launch (start us, length us, event | category | flops | bytes accessed | tf_op | source)
XLA Modules:
  0.0 1437.3 jit_solution(13607261294491723738)
XLA Ops:
  7.2 1.0 convolution_bitcast_fusion.3
  8.2 0.9 fusion.13
  9.2 1.1 convolution_add_fusion
  10.3 0.4 fusion.1
  10.7 0.6 copy.34
  11.4 0.9 convolution_convert_fusion
  12.4 1.3 broadcast_multiply_fusion
  13.9 35.5 %all_gather.7 = bf16[256,1024]{1,0:T(8,128)(2,1)S(1)} all-gather(bf16[256,128]{1,0:T(8,128)(2,1)S(1)} %copy-done.1), channel_id=1, replica_groups=mesh['patch'=64,'band'=8] {'band'}, dimensions={1}, use_global_device_ids=true | all-gather | bytes 589824 | tf_op jit(solution)/shard_map/all_gather | solution.py:75
  49.5 0.4 convolution_bitcast_fusion
  49.9 2.3 copy.23
  52.3 272.4 %all-gather.2.cloned.1.call-done = bf16[2,1024,256]{2,1,0:T(8,128)(2,1)} async-done(((bf16[2,16,256]{2,1,0:T(8,128)(2,1)}), bf16[2,1024,256]{2,1,0:T(8,128)(2,1)}) %all-gather.2.cloned.1.call-update) | async-done | bytes 1048592 | tf_op jit(solution)/shard_map/all_gather | solution.py:70
  324.7 1.7 fusion
  326.4 1.0 copy.27
  327.5 1.3 dynamic-slice
  329.4 724.8 %all-reduce.5.cloned.1.call-done = f32[1024,2,256]{2,1,0:T(2,128)} async-done(((f32[1024,2,256]{2,1,0:T(2,128)}), f32[1024,2,256]{2,1,0:T(2,128)}) %all-reduce.5.cloned.1.call-update) | async-done | bytes 2097168
  1054.3 2.0 convolution_bitcast_fusion.2
  1056.3 162.8 %psum.29 = f32[2,128]{1,0:T(2,128)S(1)} all-reduce(f32[2,128]{1,0:T(2,128)S(1)} %convolution_bitcast_fusion.2), channel_id=1, replica_groups=mesh['patch'=64,'band'=8] {'patch'}, use_global_device_ids=true, to_apply=%region_3.4 | all-reduce | flops 256 | bytes 2048 | tf_op jit(solution)/shard_map/psum | solution.py:86
  1219.1 1.0 fusion.20
  1220.1 3.1 fusion.7
  1223.5 90.2 %psum.31 = f32[4,128]{1,0:T(4,128)} all-reduce(f32[4,128]{1,0:T(4,128)S(1)} %fusion.12), channel_id=1, replica_groups=mesh['patch'=64,'band'=8] {'band'}, use_global_device_ids=true, to_apply=%region_5.6 | all-reduce | flops 512 | bytes 4096 | tf_op jit(solution)/shard_map/psum | solution.py:90
  1313.7 1.6 copy.28
  1315.3 110.7 %all-reduce.7.cloned.1.call-done = (f32[128,16,256]{2,0,1:T(8,128)}, f32[128,128]{1,0:T(8,128)}) async-done(((f32[128,16,256]{2,0,1:T(8,128)}, f32[128,128]{1,0:T(8,128)}), (f32[128,16,256]{2,0,1:T(8,128)}, f32[128,128]{1,0:T(8,128)})) %all-reduce.7.cloned.1.call-update) | async-done | bytes 2162704 | tf_op jit(solution)/shard_map/psum | solution.py:84
  1426.0 4.2 copy.25
  1430.1 0.6 copy.38
  (23 shorter events, 0.9 us)
Async XLA Ops:
  7.2 3.1 copy-start
  7.2 6.8 copy-start.1
  7.2 317.5 %all-gather.2.cloned.1.call-start = ((), (), s32[]{:S(2)}) async-start(), calls=%async_computation.1 | async-start | bytes 1064960 | tf_op jit(solution)/shard_map/all_gather | solution.py:70
  11.3 1043.0 %all-reduce.5.cloned.1.call-start = ((), (), s32[]{:S(2)}) async-start(), calls=%async_computation.3 | async-start | bytes 4194304
  52.3 1261.4 %reduce-scatter.4.cloned.1.call-start = ((), (), s32[]{:S(2)}) async-start(), calls=%async_computation.2 | async-start | bytes 589824
  327.5 1098.5 %all-reduce.7.cloned.1.call-start = ((), (), s32[]{:S(2)}) async-start(), calls=%async_computation.4 | async-start | bytes 4325376 | tf_op jit(solution)/shard_map/psum | solution.py:84
  1220.1 3.2 copy-start.3
  1426.0 4.2 copy-start.2
Sparse Core Ops, SparseCore 0:
  11.4 313.2 all-gather.1
  328.2 726.0 all-reduce.4
  1057.3 94.8 reduce-scatter.3
  1223.4 202.5 all-reduce.6
where the time goes:
time: 1440 us
  waiting for transfers between devices  1110 us (77%)
  blocking collectives  289 us (20%)
  between operations  14.5 us (1%)
    unnamed x6, waiting for transfers between devices  725 us
    all_gather x1, waiting for transfers between devices, local(): lax.all_gather(kernel_part, 'patch', axis=1, tiled=True)  272 us
    psum x1, blocking collectives, local(): grad_hidden = lax.psum(part_hidden, 'patch')  163 us
    psum x1, waiting for transfers between devices, local(): grad_out = lax.psum(part_out, 'band')  111 us
    psum x1, blocking collectives, local(): grad_first, grad_sensor = lax.psum((first_part, sensor_part), 'band')  90.2 us
    all_gather x1, blocking collectives, local(): full_cot = lax.all_gather(cotangent, 'band', axis=1, tiled=True)  35.5 us
  transfers between devices with their start and end apart: 4, of which 3 were waited for; matrix products, arithmetic and copies ran while one was open for 1% of the time, Pallas kernels for 0%

commit v1 on v0

v1 whole, which is shorter than its diff:
```python
import functools
import math

import jax
import jax.numpy as jnp
from jax import lax
from jax.experimental import pallas as pl
from jax.experimental.pallas import tpu as pltpu
from jax.sharding import Mesh
from jax.sharding import PartitionSpec as P

TILE_PATCHES = 1024
X, Y, L, H, C = 4, 4, 4, 4, 2
BD = 2
DS = 16
P2 = 256
HID = 128
BF = jnp.bfloat16
F32 = jnp.float32
HIGHEST = lax.Precision.HIGHEST
VMEM = pl.BlockSpec(memory_space=pltpu.VMEM)
SMEM = pl.BlockSpec(memory_space=pltpu.SMEM)


def call(body, shape, dtype, specs, *args, flops=0, nbytes=2**20):
    return pl.pallas_call(
        body,
        out_shape=jax.ShapeDtypeStruct(shape, dtype),
        in_specs=specs,
        out_specs=VMEM,
        compiler_params=pltpu.CompilerParams(vmem_limit_bytes=24 * 2**20),
        cost_estimate=pl.CostEstimate(flops=flops, bytes_accessed=nbytes, transcendentals=0),
    )(*args)


def iota(shape, dim):
    return lax.broadcasted_iota(jnp.int32, shape, dim)


def wave_features(waves, width):
    half = width // 2
    steps = jnp.arange(half, dtype=F32)
    freqs = jnp.exp(steps * (math.log(100.0) / half))
    angles = waves[:, None] * freqs[None, :]
    return jnp.concatenate([jnp.sin(angles), jnp.cos(angles)], axis=1)


def silu_slope(preact):
    sigma = jax.nn.sigmoid(preact)
    return sigma * (1.0 + preact * (1.0 - sigma))


def hypernet(band_index, band_sensor, wave_table, first_weight, sensor_embed):
    table_hot = (
        band_index[:, None] == jnp.arange(wave_table.shape[0], dtype=jnp.int32)[None, :]
    ).astype(F32)
    waves = jnp.dot(table_hot, wave_table, precision=HIGHEST)
    features = wave_features(waves, first_weight.shape[0])
    sensor_hot = (
        band_sensor[:, None] == jnp.arange(sensor_embed.shape[0], dtype=jnp.int32)[None, :]
    ).astype(F32)
    preact = jnp.dot(features, first_weight, precision=HIGHEST) + jnp.dot(
        sensor_hot, sensor_embed, precision=HIGHEST
    )
    return (features, sensor_hot, preact)


def kernel_body(idx, sens, table, first, sensor, weight, out):
    lane = iota((8, HID), 1)
    half = HID // 2
    step = jnp.where(lane < half, lane, lane - half).astype(F32)
    freqs = jnp.exp(step * (math.log(100.0) / half))
    row = iota((8, HID), 0)
    waves = jnp.where(row == 0, table[idx[0]], table[idx[1]])
    angles = waves * freqs
    features = jnp.where(lane < half, jnp.sin(angles), jnp.cos(angles))
    preact = jnp.dot(features, first[...], precision=HIGHEST, preferred_element_type=F32)
    preact = preact + jnp.where(row == 0, sensor[pl.ds(sens[0], 1), :], sensor[pl.ds(sens[1], 1), :])
    hidden = (preact / (1.0 + jnp.exp(-preact))).astype(BF)
    wide = (iota((HID, HID * DS), 1) // DS == iota((HID, HID * DS), 0)).astype(F32).astype(BF)
    spread = jnp.dot(hidden, wide, preferred_element_type=F32)
    own = iota((DS, HID * DS), 1) % DS == iota((DS, HID * DS), 0)
    left = jnp.concatenate([jnp.where(own, spread[c : c + 1], 0.0) for c in range(BD)], axis=0).astype(BF)
    out[...] = jnp.dot(left, weight[...], preferred_element_type=F32).astype(BF)


def embed_body(masked, kernels, out):
    for b in range(H * C):
        total = None
        for c in range(BD):
            right = kernels[8 * b : 8 * b + 8, c].reshape(8 * DS, P2)
            term = lax.dot_general(
                masked[:, c * P2 : (c + 1) * P2], right, (((1,), (1,)), ((), ())), preferred_element_type=F32
            )
            total = term if total is None else total + term
        out[b] = total.astype(BF)


def grad_body(cot, masked, out):
    for b in range(H * C):
        block = cot[b % C, b // C, 0:256, :]
        part = lax.dot_general(block, masked[...], (((0,), (0,)), ((), ())), preferred_element_type=F32).astype(BF)
        for c in range(BD):
            out[8 * b : 8 * b + 8, c] = part[:, c * P2 : (c + 1) * P2].reshape(8, DS, P2)


def sum_xy_body(parts, out):
    total = parts[0].astype(F32)
    for i in range(1, X * Y):
        total = total + parts[i].astype(F32)
    total = total.astype(BF)
    for h in range(H):
        out[:, h] = total


def sum_l_body(parts, out):
    total = parts[0].astype(F32)
    for i in range(1, L):
        total = total + parts[i].astype(F32)
    out[...] = total.astype(BF)


def hidden_grad_body(grads, weight, out):
    rows = HID * DS
    n = H * C * BD * DS
    prod = lax.dot_general(weight[...], grads[...], (((1,), (1,)), ((), ())), preferred_element_type=F32)
    keep = iota((rows, n), 0) % DS == iota((rows, n), 1) % DS
    prod = jnp.where(keep, prod, 0.0).reshape(HID, DS, n).sum(axis=1)
    pick = (iota((n // DS, n), 1) // DS == iota((n // DS, n), 0)).astype(F32)
    out[...] = lax.dot_general(pick, prod, (((1,), (1,)), ((), ())), precision=HIGHEST, preferred_element_type=F32)


def out_grad_body(hidden_t, grads, out):
    n = H * C * BD * DS
    wide = (iota((n // DS, n), 1) // DS == iota((n // DS, n), 0)).astype(F32).astype(BF)
    spread = jnp.dot(hidden_t[...], wide, preferred_element_type=F32)
    keep = iota((DS, n), 0) == iota((DS, n), 1) % DS
    left = jnp.where(keep[None], spread[:, None, :], 0.0).reshape(HID * DS, n).astype(BF)
    out[...] = jnp.dot(left, grads[...], preferred_element_type=F32)


def gather(part, axes, count):
    return lax.all_to_all(jnp.broadcast_to(part[None], (count, *part.shape)), axes, 0, 0, tiled=True)


def local(
    pixels, cotangent, avail, band_index, band_sensor, wave_table, first_weight, sensor_embed, out_weight
):
    rows = pixels.shape[0]
    place = (lax.axis_index("x") * Y + lax.axis_index("y")) * L + lax.axis_index("l")
    tile = (place * rows) // TILE_PATCHES
    mask = lax.dynamic_slice_in_dim(avail, tile, 1, 0).astype(BF)
    masked = (pixels * mask[:, :, None]).reshape(rows, BD * P2)
    weight = out_weight.reshape(HID * DS, P2)

    ids = jnp.concatenate([band_index, band_sensor]).astype(BF)
    tail = jnp.pad(ids[None], ((0, 15), (0, cotangent.shape[1] - 2 * BD)))
    cot_h = gather(jnp.concatenate([cotangent, tail], axis=0), "h", H)
    cot = lax.all_gather(cot_h, "c", axis=0, tiled=False)

    part = call(
        kernel_body, (BD * DS, P2), BF, [SMEM, SMEM, SMEM, VMEM, VMEM, VMEM],
        band_index, band_sensor, wave_table, first_weight, sensor_embed, weight, flops=2**25,
    )
    part_l = gather(part, "l", L)
    kernels = gather(part_l.reshape(L * BD * DS, P2), ("x", "y"), X * Y).reshape(X * Y * L, BD, DS, P2)
    shares = call(embed_body, (H * C, rows, 128), BF, [VMEM, VMEM], masked, kernels, flops=2**28)
    embed = lax.psum_scatter(shares, ("h", "c"), scatter_dimension=0, tiled=False)

    grads = call(grad_body, (X * Y * L, BD, DS, P2), BF, [VMEM, VMEM], cot, masked, flops=2**28)
    grads = lax.all_to_all(grads.reshape(X * Y, L, BD * DS, P2), ("x", "y"), 0, 0, tiled=True)
    grads = call(sum_xy_body, (L, H, BD * DS, P2), BF, [VMEM], grads, flops=2**20)
    grads = lax.all_to_all(grads.reshape(L * H, BD * DS, P2), ("l", "h"), 0, 0, tiled=True)
    grads = call(sum_l_body, (H, BD * DS, P2), BF, [VMEM], grads.reshape(L, H, BD * DS, P2), flops=2**18)
    grads = lax.all_gather(grads, "c", axis=0, tiled=False).reshape(C * H * BD * DS, P2)

    every = cot[:, :, rows, : 2 * BD].astype(jnp.int32).reshape(C * H, 2 * BD)
    features, sensor_hot, preact = hypernet(
        every[:, :BD].reshape(-1), every[:, BD:].reshape(-1), wave_table, first_weight, sensor_embed
    )
    hidden_t = jax.nn.silu(preact).astype(BF).T
    slope = silu_slope(preact)

    part_hidden = call(hidden_grad_body, (C * H * BD, HID), F32, [VMEM, VMEM], grads, weight, flops=2**28)
    grad_hidden = gather(part_hidden, ("x", "y"), X * Y).sum(axis=0)
    grad_hidden = gather(grad_hidden, "l", L).sum(axis=0)
    grad_out = call(out_grad_body, (HID * DS, P2), F32, [VMEM, VMEM], hidden_t, grads, flops=2**28)
    grad_pre = grad_hidden * slope
    grad_first = jnp.dot(features.T, grad_pre, precision=HIGHEST)
    grad_sensor = jnp.dot(sensor_hot.T, grad_pre, precision=HIGHEST)
    return (embed, grad_out.reshape(HID, DS, P2), grad_first, grad_sensor)


def solution(mesh):
    fine = Mesh(mesh.devices.reshape(X, Y, L, H, C), ("x", "y", "l", "h", "c"))
    patch, band = ("x", "y", "l"), ("h", "c")
    return jax.shard_map(
        local,
        mesh=fine,
        in_specs=(
            P(patch, band, None),
            P(patch, band),
            P(None, band),
            P(band),
            P(band),
            P(),
            P(),
            P(),
            P(None, patch, None),
        ),
        out_specs=(P(patch, band), P(None, patch, None), P(), P()),
        check_vma=False,
    )
```

time: 1440 us -> 167 us (0.12)
  waiting for transfers between devices: 1110 us -> 49.5 us
  blocking collectives: 289 us -> 32.3 us
  starting transfers between devices: 0.16 us -> 49.4 us
    unnamed x6 -> x1, waiting for transfers between devices: 725 us -> 0.02 us
    all_gather x1 -> x0, waiting for transfers between devices: 272 us -> none  [local(): lax.all_gather(kernel_part, 'patch', axis=1, tiled=True)]
    psum x2 -> x0, blocking collectives: 253 us -> none  [the longest x1 163 us: local(): grad_hidden = lax.psum(part_hidden, 'patch')]
    psum x1 -> x0, waiting for transfers between devices: 111 us -> none  [local(): grad_out = lax.psum(part_out, 'band')]
    all_to_all x0 -> x6, starting transfers between devices: none -> 49.3 us  [the longest x5 36.7 us: gather(): lax.all_to_all(jnp.broadcast_to(part[None], (count, *part.shape)), axes,...]
    all_to_all x0 -> x6, waiting for transfers between devices: none -> 38.9 us  [the longest x5 27.3 us: gather(): lax.all_to_all(jnp.broadcast_to(part[None], (count, *part.shape)), axes,...]
    all_gather x1 -> x2, blocking collectives: 35.5 us -> 12.5 us  [the longest x1 7.78 us: local(): lax.all_gather(grads, 'c', axis=0, tiled=False).reshape(C * H * BD * DS, P2)]
    all_to_all x0 -> x1, blocking collectives: none -> 19.8 us  [local(): lax.all_to_all(grads.reshape(X * Y, L, BD * DS, P2), ('x', 'y'), 0, 0, ti...]
  transfers between devices with their start and end apart: 4 -> 7, of which waited for: 3 -> 6; matrix products, arithmetic and copies ran while one was open for 1% -> 3% of each run, Pallas kernels for 0% -> 4%
where the time goes in v1:
time: 167 us
  waiting for transfers between devices  49.5 us (30%)
  starting transfers between devices  49.4 us (30%)
  blocking collectives  32.3 us (19%)
  between operations  14.2 us (9%)
  local copies, waits for them, and re-layouts  8.9 us (5%)
  Pallas kernels  6.85 us (4%)
  other arithmetic  3 us (2%)
  matrix products  2.42 us (1%)
    all_to_all x5, starting transfers between devices, gather(): lax.all_to_all(jnp.broadcast_to(part[None], (count, *part.shape)), axes,...  36.7 us
    all_to_all x5, waiting for transfers between devices, gather(): lax.all_to_all(jnp.broadcast_to(part[None], (count, *part.shape)), axes,...  27.3 us
    all_to_all x1, blocking collectives, local(): lax.all_to_all(grads.reshape(X * Y, L, BD * DS, P2), ('x', 'y'), 0, 0, ti...  19.8 us
    all_to_all x1, starting transfers between devices, local(): lax.all_to_all(grads.reshape(L * H, BD * DS, P2), ('l', 'h'), 0, 0, tiled...  12.6 us
    all_to_all x1, waiting for transfers between devices, local(): lax.all_to_all(grads.reshape(L * H, BD * DS, P2), ('l', 'h'), 0, 0, tiled...  11.7 us
    reduce_scatter x1, waiting for transfers between devices, local(): lax.psum_scatter(shares, ('h', 'c'), scatter_dimension=0, tiled=False)  10.6 us
    all_gather x1, blocking collectives, local(): lax.all_gather(grads, 'c', axis=0, tiled=False).reshape(C * H * BD * DS, P2)  7.78 us
    pallas_call x7, Pallas kernels, call(): pl.pallas_call(body, out_shape=jax.ShapeDtypeStruct(shape, dtype), in_spe...  6.85 us
  transfers between devices with their start and end apart: 7, of which 6 were waited for; matrix products, arithmetic and copies ran while one was open for 3% of the time, Pallas kernels for 4%

profile of v1, /device:TPU:1, one launch (start us, length us, event | category | flops | bytes accessed | tf_op | source)
XLA Modules:
  0.0 166.5 jit_solution(12451250792553780792)
XLA Ops:
  8.0 0.8 pad_maximum_fusion
  9.6 15.6 %all-to-all-start.2 = ((bf16[4,272,128]{2,1,0:T(8,128)(2,1)}), bf16[4,272,128]{2,1,0:T(8,128)(2,1)S(1)}, u32[]{:S(2)}, u32[]{:S(2)}) async-start(bf16[4,272,128]{2,1,0:T(8,128)(2,1)} %broadcast_in_dim.15), calls=%async_computation.3 | async-start | bytes 557056 | tf_op jit(solution)/shard_map/all_to_all | solution.py:143
  25.2 0.9 fusion.16
  26.1 1.2 copy-done
  30.8 1.2 shard_map.120
  32.0 7.2 %all-to-all-done.2 = bf16[4,272,128]{2,1,0:T(8,128)(2,1)S(1)} async-done(((bf16[4,272,128]{2,1,0:T(8,128)(2,1)}), bf16[4,272,128]{2,1,0:T(8,128)(2,1)S(1)}, u32[]{:S(2)}, u32[]{:S(2)}) %all-to-all-start.2) | async-done | bytes 278560 | tf_op jit(solution)/shard_map/all_to_all | solution.py:143
  39.8 8.5 %all-to-all-start = ((bf16[4,32,256]{2,1,0:T(8,128)(2,1)}), bf16[4,32,256]{2,1,0:T(8,128)(2,1)S(1)}, u32[]{:S(2)}, u32[]{:S(2)}) async-start(bf16[4,32,256]{2,1,0:T(8,128)(2,1)} %broadcast_in_dim.12), calls=%async_computation | async-start | bytes 131072 | tf_op jit(solution)/shard_map/all_to_all | solution.py:143
  48.6 4.7 %all-gather = bf16[8,272,128]{2,1,0:T(8,128)(2,1)S(1)} all-gather(bf16[4,272,128]{2,1,0:T(8,128)(2,1)S(1)} %all-to-all-done.2), channel_id=2, replica_groups=mesh['x'=4,'y'=4,'l'=4,'h'=4,'c'=2] {'c'}, dimensions={0}, use_global_device_ids=true | all-gather | bytes 835584 | tf_op jit(solution)/shard_map/all_gather | solution.py:159
  53.8 19.8 %all_to_all.35.parts = bf16[16,4,32,256]{3,2,1,0:T(8,128)(2,1)S(1)} all-to-all(bf16[16,4,32,256]{3,2,1,0:T(8,128)(2,1)S(1)} %bitcast.37), channel_id=1, replica_groups=mesh['x'=4,'y'=4,'l'=4,'h'=4,'c'=2] {'x','y'}, dimensions={0} | all-to-all | bytes 2097152 | tf_op jit(solution)/shard_map/all_to_all | solution.py:171
  73.6 1.1 broadcast_in_dim.14
  74.7 3.8 %all-to-all-start.1 = ((bf16[16,128,256]{2,1,0:T(8,128)(2,1)}), bf16[16,128,256]{2,1,0:T(8,128)(2,1)S(1)}, u32[]{:S(2)}, u32[]{:S(2)}) async-start(bf16[16,128,256]{2,1,0:T(8,128)(2,1)} %broadcast_in_dim.14), calls=%async_computation.1 | async-start | bytes 2097152 | tf_op jit(solution)/shard_map/all_to_all | solution.py:143
  79.4 11.1 %all-to-all-done.1 = bf16[16,128,256]{2,1,0:T(8,128)(2,1)S(1)} async-done(((bf16[16,128,256]{2,1,0:T(8,128)(2,1)}), bf16[16,128,256]{2,1,0:T(8,128)(2,1)S(1)}, u32[]{:S(2)}, u32[]{:S(2)}) %all-to-all-start.1) | async-done | bytes 1048608 | tf_op jit(solution)/shard_map/all_to_all | solution.py:143
  90.4 12.6 %all-to-all-start.4 = ((bf16[16,32,256]{2,1,0:T(8,128)(2,1)}), bf16[16,32,256]{2,1,0:T(8,128)(2,1)S(1)}, u32[]{:S(2)}, u32[]{:S(2)}) async-start(bf16[16,32,256]{2,1,0:T(8,128)(2,1)} %bitcast.12), calls=%async_computation.5 | async-start | bytes 524288 | tf_op jit(solution)/shard_map/all_to_all | solution.py:173
  103.6 1.5 shard_map.121
  105.4 11.7 %all-to-all-done.4 = bf16[16,32,256]{2,1,0:T(8,128)(2,1)S(1)} async-done(((bf16[16,32,256]{2,1,0:T(8,128)(2,1)}), bf16[16,32,256]{2,1,0:T(8,128)(2,1)S(1)}, u32[]{:S(2)}, u32[]{:S(2)}) %all-to-all-start.4) | async-done | bytes 262176 | tf_op jit(solution)/shard_map/all_to_all | solution.py:173
  117.1 7.8 %all-gather.1 = bf16[8,32,256]{2,1,0:T(8,128)(2,1)S(1)} all-gather(bf16[4,32,256]{2,1,0:T(8,128)(2,1)S(1)} %shard_map.124), channel_id=3, replica_groups=mesh['x'=4,'y'=4,'l'=4,'h'=4,'c'=2] {'c'}, dimensions={0}, use_global_device_ids=true | all-gather | bytes 196608 | tf_op jit(solution)/shard_map/all_gather | solution.py:175
  124.9 1.0 shard_map.126
  126.6 3.7 %all-to-all-start.5 = ((f32[16,16,128]{2,1,0:T(8,128)}), f32[16,16,128]{2,1,0:T(8,128)S(1)}, u32[]{:S(2)}, u32[]{:S(2)}) async-start(f32[16,16,128]{2,1,0:T(8,128)} %broadcast_in_dim.16), calls=%async_computation.6 | async-start | bytes 262144 | tf_op jit(solution)/shard_map/all_to_all | solution.py:143
  130.6 6.4 %all-to-all-done.5 = f32[16,16,128]{2,1,0:T(8,128)S(1)} async-done(((f32[16,16,128]{2,1,0:T(8,128)}), f32[16,16,128]{2,1,0:T(8,128)S(1)}, u32[]{:S(2)}, u32[]{:S(2)}) %all-to-all-start.5) | async-done | bytes 131104 | tf_op jit(solution)/shard_map/all_to_all | solution.py:143
  137.6 5.1 %all-to-all-start.6 = ((f32[4,16,128]{2,1,0:T(8,128)}), f32[4,16,128]{2,1,0:T(8,128)S(1)}, u32[]{:S(2)}, u32[]{:S(2)}) async-start(f32[4,16,128]{2,1,0:T(8,128)} %broadcast_in_dim.17), calls=%async_computation.7 | async-start | bytes 65536 | tf_op jit(solution)/shard_map/all_to_all | solution.py:143
  142.7 1.9 %shard_map.125 = f32[2048,256]{1,0:T(8,128)} custom-call(bf16[128,16]{1,0:T(8,128)(2,1)S(1)} %fusion.3.hidden_t, bf16[256,256]{1,0:T(8,128)(2,1)S(1)} %bitcast.45), custom_call_target="tpu_custom_call" | custom-call | flops 268435456 | bytes 1048576 | tf_op jit(solution)/shard_map/pallas_call | solution.py:26
  144.6 2.6 %all-to-all-done.6 = f32[4,16,128]{2,1,0:T(8,128)S(1)} async-done(((f32[4,16,128]{2,1,0:T(8,128)}), f32[4,16,128]{2,1,0:T(8,128)S(1)}, u32[]{:S(2)}, u32[]{:S(2)}) %all-to-all-start.6) | async-done | bytes 32800 | tf_op jit(solution)/shard_map/all_to_all | solution.py:143
  148.1 1.0 fusion.14
  149.1 10.6 %reduce-scatter.2.cloned.1.call-done = bf16[1,256,128]{2,1,0:T(8,128)(2,1)} async-done(((bf16[8,256,128]{2,1,0:T(8,128)(2,1)}), bf16[1,256,128]{2,1,0:T(8,128)(2,1)}) %reduce-scatter.2.cloned.1.call-update) | async-done | bytes 65552 | tf_op jit(solution)/shard_map/reduce_scatter | solution.py:168
  (49 shorter events, 10.7 us)
Async XLA Ops:
  7.2 41.1 %copy-start.10 = (bf16[256,2,256]{2,1,0:T(2,128)(2,1)S(1)}, bf16[256,2,256]{2,1,0:T(2,128)(2,1)}, u32[]{:S(2)}) copy-start(bf16[256,2,256]{2,1,0:T(2,128)(2,1)} %param.9) | copy-start | bytes 786436
  9.6 29.6 %all-to-all-start.2 = ((bf16[4,272,128]{2,1,0:T(8,128)(2,1)}), bf16[4,272,128]{2,1,0:T(8,128)(2,1)S(1)}, u32[]{:S(2)}, u32[]{:S(2)}) async-start(bf16[4,272,128]{2,1,0:T(8,128)(2,1)} %broadcast_in_dim.15), calls=%async_computation.3 | async-start | bytes 557056 | tf_op jit(solution)/shard_map/all_to_all | solution.py:143
  26.1 1.2 copy-start
  27.3 0.8 copy-start.2
  28.1 0.7 copy-start.4
  28.8 0.7 copy-start.6
  29.5 0.7 copy-start.7
  30.1 0.7 copy-start.8
  39.8 14.0 %all-to-all-start = ((bf16[4,32,256]{2,1,0:T(8,128)(2,1)}), bf16[4,32,256]{2,1,0:T(8,128)(2,1)S(1)}, u32[]{:S(2)}, u32[]{:S(2)}) async-start(bf16[4,32,256]{2,1,0:T(8,128)(2,1)} %broadcast_in_dim.12), calls=%async_computation | async-start | bytes 131072 | tf_op jit(solution)/shard_map/all_to_all | solution.py:143
  74.7 28.6 %copy-start.9 = (f32[208]{0:T(256)S(1)}, f32[208]{0:T(256)}, u32[]{:S(2)}) copy-start(f32[208]{0:T(256)} %table.1) | copy-start | bytes 2500
  74.7 15.8 %all-to-all-start.1 = ((bf16[16,128,256]{2,1,0:T(8,128)(2,1)}), bf16[16,128,256]{2,1,0:T(8,128)(2,1)S(1)}, u32[]{:S(2)}, u32[]{:S(2)}) async-start(bf16[16,128,256]{2,1,0:T(8,128)(2,1)} %broadcast_in_dim.14), calls=%async_computation.1 | async-start | bytes 2097152 | tf_op jit(solution)/shard_map/all_to_all | solution.py:143
  78.5 26.6 %copy-start.3 = (f32[128,128]{1,0:T(8,128)S(1)}, f32[128,128]{1,0:T(8,128)}, u32[]{:S(2)}) copy-start(f32[128,128]{1,0:T(8,128)} %first.1) | copy-start | bytes 196612
  79.4 45.5 %copy-start.1 = (bf16[128,16,256]{2,1,0:T(8,128)(2,1)S(1)}, bf16[128,16,256]{2,1,0:T(8,128)(2,1)}, u32[]{:S(2)}) copy-start(bf16[128,16,256]{2,1,0:T(8,128)(2,1)} %param.17) | copy-start | bytes 3145732
  90.4 26.6 %all-to-all-start.4 = ((bf16[16,32,256]{2,1,0:T(8,128)(2,1)}), bf16[16,32,256]{2,1,0:T(8,128)(2,1)S(1)}, u32[]{:S(2)}, u32[]{:S(2)}) async-start(bf16[16,32,256]{2,1,0:T(8,128)(2,1)} %bitcast.12), calls=%async_computation.5 | async-start | bytes 524288 | tf_op jit(solution)/shard_map/all_to_all | solution.py:173
  103.0 56.6 %reduce-scatter.2.cloned.1.call-start = ((), (), s32[]{:S(2)}) async-start(), calls=%async_computation.8 | async-start | bytes 589824 | tf_op jit(solution)/shard_map/reduce_scatter | solution.py:168
  103.6 26.7 %copy-start.5 = (f32[4,128]{1,0:T(4,128)S(1)}, f32[4,128]{1,0:T(4,128)}, u32[]{:S(2)}) copy-start(f32[4,128]{1,0:T(4,128)} %sensor.1) | copy-start | bytes 6148
  126.6 10.4 %all-to-all-start.5 = ((f32[16,16,128]{2,1,0:T(8,128)}), f32[16,16,128]{2,1,0:T(8,128)S(1)}, u32[]{:S(2)}, u32[]{:S(2)}) async-start(f32[16,16,128]{2,1,0:T(8,128)} %broadcast_in_dim.16), calls=%async_computation.6 | async-start | bytes 262144 | tf_op jit(solution)/shard_map/all_to_all | solution.py:143
  137.6 9.6 %all-to-all-start.6 = ((f32[4,16,128]{2,1,0:T(8,128)}), f32[4,16,128]{2,1,0:T(8,128)S(1)}, u32[]{:S(2)}, u32[]{:S(2)}) async-start(f32[4,16,128]{2,1,0:T(8,128)} %broadcast_in_dim.17), calls=%async_computation.7 | async-start | bytes 65536 | tf_op jit(solution)/shard_map/all_to_all | solution.py:143
Sparse Core Ops, SparseCore 0:
  107.3 52.3 reduce-scatter.1

commit v2 on v1

--- a/solution.py
+++ b/solution.py
@@ -22,13 +22,13 @@
 SMEM = pl.BlockSpec(memory_space=pltpu.SMEM)
 
 
-def call(body, shape, dtype, specs, *args, flops=0, nbytes=2**20):
+def call(body, outs, specs, *args, flops=0, nbytes=2**20, vmem=24):
     return pl.pallas_call(
         body,
-        out_shape=jax.ShapeDtypeStruct(shape, dtype),
+        out_shape=[jax.ShapeDtypeStruct(shape, dtype) for shape, dtype in outs],
         in_specs=specs,
-        out_specs=VMEM,
-        compiler_params=pltpu.CompilerParams(vmem_limit_bytes=24 * 2**20),
+        out_specs=[VMEM] * len(outs),
+        compiler_params=pltpu.CompilerParams(vmem_limit_bytes=vmem * 2**20),
         cost_estimate=pl.CostEstimate(flops=flops, bytes_accessed=nbytes, transcendentals=0),
     )(*args)
 
@@ -81,19 +81,35 @@
     spread = jnp.dot(hidden, wide, preferred_element_type=F32)
     own = iota((DS, HID * DS), 1) % DS == iota((DS, HID * DS), 0)
     left = jnp.concatenate([jnp.where(own, spread[c : c + 1], 0.0) for c in range(BD)], axis=0).astype(BF)
-    out[...] = jnp.dot(left, weight[...], preferred_element_type=F32).astype(BF)
-
-
-def embed_body(masked, kernels, out):
-    for b in range(H * C):
-        total = None
-        for c in range(BD):
-            right = kernels[8 * b : 8 * b + 8, c].reshape(8 * DS, P2)
-            term = lax.dot_general(
-                masked[:, c * P2 : (c + 1) * P2], right, (((1,), (1,)), ((), ())), preferred_element_type=F32
-            )
-            total = term if total is None else total + term
-        out[b] = total.astype(BF)
+    part = jnp.dot(left, weight[...], preferred_element_type=F32).astype(BF)
+    for to in range(L):
+        out[to] = part
+
+
+def embed_body(masked, kernels, keep, send):
+    core, high = lax.axis_index("c"), lax.axis_index("h")
+    for step in range(H):
+        to = lax.rem(high + step, H)
+        for out, side in ((keep, core), (send, 1 - core)):
+            first = 8 * (to * C + side)
+            total = None
+            for c in range(BD):
+                right = kernels[pl.ds(first, 8), c].reshape(8 * DS, P2)
+                term = lax.dot_general(
+                    masked[:, c * P2 : (c + 1) * P2], right, (((1,), (1,)), ((), ())), preferred_element_type=F32
+                )
+                total = term if total is None else total + term
+            out[step] = total.astype(BF)
+
+
+def pair_body(keep, other, *outs):
+    for step in range(H):
+        outs[step][...] = (keep[step].astype(F32) + other[step].astype(F32)).astype(BF)
+
+
+def join_body(a, b, c, d, out):
+    total = a[...].astype(F32) + b[...].astype(F32)
+    out[...] = (total + c[...].astype(F32) + d[...].astype(F32)).astype(BF)
 
 
 def grad_body(cot, masked, out):
@@ -122,12 +138,32 @@
 
 def hidden_grad_body(grads, weight, out):
     rows = HID * DS
-    n = H * C * BD * DS
+    n = H * BD * DS
     prod = lax.dot_general(weight[...], grads[...], (((1,), (1,)), ((), ())), preferred_element_type=F32)
     keep = iota((rows, n), 0) % DS == iota((rows, n), 1) % DS
     prod = jnp.where(keep, prod, 0.0).reshape(HID, DS, n).sum(axis=1)
     pick = (iota((n // DS, n), 1) // DS == iota((n // DS, n), 0)).astype(F32)
-    out[...] = lax.dot_general(pick, prod, (((1,), (1,)), ((), ())), precision=HIGHEST, preferred_element_type=F32)
+    part = lax.dot_general(pick, prod, (((1,), (1,)), ((), ())), precision=HIGHEST, preferred_element_type=F32)
+    for to in range(X * Y):
+        out[to] = part
+
+
+def spread_body(parts, out):
+    total = parts[0]
+    for i in range(1, X * Y):
+        total = total + parts[i]
+    for to in range(L * C):
+        out[to] = total
+
+
+def final_body(parts, slope, features, sensor_hot, first, sensor):
+    total = parts[0]
+    for i in range(1, L):
+        total = total + parts[i]
+    grad_pre = total * slope[...]
+    across = (((0,), (0,)), ((), ()))
+    first[...] = lax.dot_general(features[...], grad_pre, across, precision=HIGHEST, preferred_element_type=F32)
+    sensor[...] = lax.dot_general(sensor_hot[...], grad_pre, across, precision=HIGHEST, preferred_element_type=F32)
 
 
 def out_grad_body(hidden_t, grads, out):
@@ -153,26 +189,37 @@
     masked = (pixels * mask[:, :, None]).reshape(rows, BD * P2)
     weight = out_weight.reshape(HID * DS, P2)
 
+    (part,) = call(
+        kernel_body, [((L, BD * DS, P2), BF)], [SMEM, SMEM, SMEM, VMEM, VMEM, VMEM],
+        band_index, band_sensor, wave_table, first_weight, sensor_embed, weight, flops=2**25, vmem=60,
+    )
+    part_l = lax.all_to_all(part, "l", 0, 0, tiled=True)
+
     ids = jnp.concatenate([band_index, band_sensor]).astype(BF)
     tail = jnp.pad(ids[None], ((0, 15), (0, cotangent.shape[1] - 2 * BD)))
-    cot_h = gather(jnp.concatenate([cotangent, tail], axis=0), "h", H)
-    cot = lax.all_gather(cot_h, "c", axis=0, tiled=False)
-
-    part = call(
-        kernel_body, (BD * DS, P2), BF, [SMEM, SMEM, SMEM, VMEM, VMEM, VMEM],
-        band_index, band_sensor, wave_table, first_weight, sensor_embed, weight, flops=2**25,
-    )
-    part_l = gather(part, "l", L)
+    cot_own = jnp.concatenate([cotangent, tail], axis=0)
+    cot_own, part_l = lax.optimization_barrier((cot_own, part_l))
     kernels = gather(part_l.reshape(L * BD * DS, P2), ("x", "y"), X * Y).reshape(X * Y * L, BD, DS, P2)
-    shares = call(embed_body, (H * C, rows, 128), BF, [VMEM, VMEM], masked, kernels, flops=2**28)
-    embed = lax.psum_scatter(shares, ("h", "c"), scatter_dimension=0, tiled=False)
-
-    grads = call(grad_body, (X * Y * L, BD, DS, P2), BF, [VMEM, VMEM], cot, masked, flops=2**28)
+    cot = lax.all_gather(lax.all_gather(cot_own, "h", axis=0, tiled=False), "c", axis=0, tiled=False)
+    (grads,) = call(grad_body, [((X * Y * L, BD, DS, P2), BF)], [VMEM, VMEM], cot, masked, flops=2**28)
+
+    grads, kernels = lax.optimization_barrier((grads, kernels))
     grads = lax.all_to_all(grads.reshape(X * Y, L, BD * DS, P2), ("x", "y"), 0, 0, tiled=True)
-    grads = call(sum_xy_body, (L, H, BD * DS, P2), BF, [VMEM], grads, flops=2**20)
+    shape = ((H, rows, 128), BF)
+    keep, send = call(embed_body, [shape, shape], [VMEM, VMEM], masked, kernels, flops=2**28)
+    other = lax.ppermute(send, "c", [(0, 1), (1, 0)])
+    shares = call(pair_body, [((rows, 128), BF)] * H, [VMEM, VMEM], keep, other, flops=2**18)
+    shares = [shares[0]] + [
+        lax.ppermute(shares[step], "h", [(i, (i + step) % H) for i in range(H)]) for step in range(1, H)
+    ]
+    (embed,) = call(join_body, [((rows, 128), BF)], [VMEM] * H, *shares, flops=2**18)
+
+    grads, *_ = lax.optimization_barrier((grads, shares[1]))
+    (grads,) = call(sum_xy_body, [((L, H, BD * DS, P2), BF)], [VMEM], grads, flops=2**20)
     grads = lax.all_to_all(grads.reshape(L * H, BD * DS, P2), ("l", "h"), 0, 0, tiled=True)
-    grads = call(sum_l_body, (H, BD * DS, P2), BF, [VMEM], grads.reshape(L, H, BD * DS, P2), flops=2**18)
-    grads = lax.all_gather(grads, "c", axis=0, tiled=False).reshape(C * H * BD * DS, P2)
+    (grads,) = call(sum_l_body, [((H, BD * DS, P2), BF)], [VMEM], grads.reshape(L, H, BD * DS, P2), flops=2**18)
+    mine = grads.reshape(H * BD * DS, P2)
+    grads = lax.all_gather(mine, "c", axis=0, tiled=True)
 
     every = cot[:, :, rows, : 2 * BD].astype(jnp.int32).reshape(C * H, 2 * BD)
     features, sensor_hot, preact = hypernet(
@@ -181,13 +228,17 @@
     hidden_t = jax.nn.silu(preact).astype(BF).T
     slope = silu_slope(preact)
 
-    part_hidden = call(hidden_grad_body, (C * H * BD, HID), F32, [VMEM, VMEM], grads, weight, flops=2**28)
-    grad_hidden = gather(part_hidden, ("x", "y"), X * Y).sum(axis=0)
-    grad_hidden = gather(grad_hidden, "l", L).sum(axis=0)
-    grad_out = call(out_grad_body, (HID * DS, P2), F32, [VMEM, VMEM], hidden_t, grads, flops=2**28)
-    grad_pre = grad_hidden * slope
-    grad_first = jnp.dot(features.T, grad_pre, precision=HIGHEST)
-    grad_sensor = jnp.dot(sensor_hot.T, grad_pre, precision=HIGHEST)
+    bands = C * H * BD
+    (parts,) = call(hidden_grad_body, [((X * Y, bands // C, HID), F32)], [VMEM, VMEM], mine, weight, flops=2**28)
+    parts = lax.all_to_all(parts, ("x", "y"), 0, 0, tiled=True)
+    parts, *_ = lax.optimization_barrier((parts, shares[3]))
+    (parts,) = call(spread_body, [((L * C, bands // C, HID), F32)], [VMEM], parts, flops=2**16)
+    parts = lax.all_to_all(parts, ("l", "c"), 0, 0, tiled=True).reshape(L, bands, HID)
+    (grad_out,) = call(out_grad_body, [((HID * DS, P2), F32)], [VMEM, VMEM], hidden_t, grads, flops=2**28)
+    grad_first, grad_sensor = call(
+        final_body, [(first_weight.shape, F32), (sensor_embed.shape, F32)], [VMEM] * 4,
+        parts, slope, features, sensor_hot, flops=2**20,
+    )
     return (embed, grad_out.reshape(HID, DS, P2), grad_first, grad_sensor)
 
 

time: 167 us -> 139 us (0.83)
  waiting for transfers between devices: 49.5 us -> 18.1 us
  starting transfers between devices: 49.4 us -> 69.9 us
  between operations: 14.2 us -> 0.87 us
  local copies, waits for them, and re-layouts: 8.9 us -> 1.5 us
  Pallas kernels: 6.85 us -> 11.3 us
  matrix products: 2.42 us -> 0.56 us
    all_to_all x0 -> x4, starting transfers between devices: none -> 36.9 us  [the longest x1 14.4 us: local(): lax.all_to_all(parts, ('l', 'c'), 0, 0, tiled=True).reshape(L, bands, HID)]
    all_to_all x5 -> x1, starting transfers between devices: 36.7 us -> 6.75 us  [gather(): lax.all_to_all(jnp.broadcast_to(part[None], (count, *part.shape)), axes,...]
    all_to_all x5 -> x1, waiting for transfers between devices: 27.3 us -> 0.01 us  [gather(): lax.all_to_all(jnp.broadcast_to(part[None], (count, *part.shape)), axes,...]
    all_to_all x1 -> x0, blocking collectives: 19.8 us -> none  [local(): lax.all_to_all(grads.reshape(X * Y, L, BD * DS, P2), ('x', 'y'), 0, 0, ti...]
    all_gather x2 -> x3, blocking collectives: 12.5 us -> 32.1 us  [the longest x1 23.3 us: local(): lax.all_gather(cot_own, 'h', axis=0, tiled=False)]
    ppermute x0 -> x4, starting transfers between devices: none -> 18.7 us  [the longest x3 16.1 us: local(): lax.ppermute(shares[step], 'h', [(i, (i + step) % H) for i in range(H)])]
    reduce_scatter x1 -> x0, waiting for transfers between devices: 10.6 us -> none  [local(): lax.psum_scatter(shares, ('h', 'c'), scatter_dimension=0, tiled=False)]
    ppermute x0 -> x4, waiting for transfers between devices: none -> 7.5 us  [the longest x3 6.37 us: local(): lax.ppermute(shares[step], 'h', [(i, (i + step) % H) for i in range(H)])]
  transfers between devices with their start and end apart: 7 -> 10, of which waited for: 6 -> 6; matrix products, arithmetic and copies ran while one was open for 3% -> 3% of each run, Pallas kernels for 4% -> 5%
where the time goes in v2:
time: 139 us; the launch traced here: 138 us
  starting transfers between devices  69.9 us (50%)
  blocking collectives  32.1 us (23%)
  waiting for transfers between devices  18.1 us (13%)
  Pallas kernels  11.3 us (8%)
  other arithmetic  3.1 us (2%)
  local copies, waits for them, and re-layouts  1.5 us (1%)
    all_gather x1, blocking collectives, local(): lax.all_gather(cot_own, 'h', axis=0, tiled=False)  23.3 us
    ppermute x3, starting transfers between devices, local(): lax.ppermute(shares[step], 'h', [(i, (i + step) % H) for i in range(H)])  16.1 us
    all_to_all x1, starting transfers between devices, local(): lax.all_to_all(parts, ('l', 'c'), 0, 0, tiled=True).reshape(L, bands, HID)  14.4 us
    pallas_call x11, Pallas kernels, call(): pl.pallas_call(body, out_shape=[jax.ShapeDtypeStruct(shape, dtype) for sh...  11.3 us
    all_to_all x1, starting transfers between devices, local(): parts = lax.all_to_all(parts, ('x', 'y'), 0, 0, tiled=True)  8.61 us
    all_to_all x1, starting transfers between devices, local(): lax.all_to_all(grads.reshape(L * H, BD * DS, P2), ('l', 'h'), 0, 0, tiled...  7.64 us
    all_to_all x1, starting transfers between devices, local(): lax.all_to_all(grads.reshape(X * Y, L, BD * DS, P2), ('x', 'y'), 0, 0, ti...  7.41 us
    all_gather x1, blocking collectives, local(): lax.all_gather(lax.all_gather(cot_own, 'h', axis=0, tiled=False), 'c', ax...  6.88 us
  transfers between devices with their start and end apart: 10, of which 6 were waited for; matrix products, arithmetic and copies ran while one was open for 3% of the time, Pallas kernels for 5%

profile of v2, /device:TPU:1, one launch (start us, length us, event | category | flops | bytes accessed | tf_op | source)
XLA Modules:
  0.0 137.5 jit_solution(15903169569463336012)
XLA Ops:
  0.7 2.6 %shard_map.120 = bf16[4,32,256]{2,1,0:T(8,128)(2,1)} custom-call(s32[2]{0:T(128)} %idx.1, s32[2]{0:T(128)} %sens.1, f32[208]{0:T(256)} %table.1, f32[128,128]{1,0:T(8,128)} %first.1, f32[4,128]{1,0:T(4,128)} %sensor.1, bf16[2048,256]{1,0:T(8,128)(2,1)} %bitcast.38), custom_call_target="tpu_custom_call" | custom-call | flops 33554432 | bytes 1048576 | tf_op jit(solution)/shard_map/pallas_call | solution.py:26
  3.3 6.4 %all-to-all-start = ((bf16[4,32,256]{2,1,0:T(8,128)(2,1)}), bf16[4,32,256]{2,1,0:T(8,128)(2,1)S(1)}, u32[]{:S(2)}, u32[]{:S(2)}) async-start(bf16[4,32,256]{2,1,0:T(8,128)(2,1)} %shard_map.120), calls=%async_computation | async-start | bytes 131072 | tf_op jit(solution)/shard_map/all_to_all | solution.py:196
  11.3 3.0 %all-to-all-done = bf16[4,32,256]{2,1,0:T(8,128)(2,1)S(1)} async-done(((bf16[4,32,256]{2,1,0:T(8,128)(2,1)}), bf16[4,32,256]{2,1,0:T(8,128)(2,1)S(1)}, u32[]{:S(2)}, u32[]{:S(2)}) %all-to-all-start) | async-done | bytes 65568 | tf_op jit(solution)/shard_map/all_to_all | solution.py:196
  14.3 1.1 broadcast_in_dim.5
  15.4 6.8 %all-to-all-start.1 = ((bf16[16,128,256]{2,1,0:T(8,128)(2,1)}), bf16[16,128,256]{2,1,0:T(8,128)(2,1)S(1)}, u32[]{:S(2)}, u32[]{:S(2)}) async-start(bf16[16,128,256]{2,1,0:T(8,128)(2,1)} %broadcast_in_dim.5), calls=%async_computation.1 | async-start | bytes 2097152 | tf_op jit(solution)/shard_map/all_to_all | solution.py:179
  22.7 23.3 %all-gather = bf16[1088,128]{1,0:T(8,128)(2,1)S(1)} all-gather(bf16[272,128]{1,0:T(8,128)(2,1)S(1)} %pad_maximum_fusion), channel_id=2, replica_groups=mesh['x'=4,'y'=4,'l'=4,'h'=4,'c'=2] {'h'}, dimensions={0}, use_global_device_ids=true | all-gather | bytes 348160 | tf_op jit(solution)/shard_map/all_gather | solution.py:203
  46.1 6.9 %all-gather.1 = bf16[8,272,128]{2,1,0:T(8,128)(2,1)S(1)} all-gather(bf16[4,272,128]{2,1,0:T(8,128)(2,1)S(1)} %bitcast.50), channel_id=3, replica_groups=mesh['x'=4,'y'=4,'l'=4,'h'=4,'c'=2] {'c'}, dimensions={0}, use_global_device_ids=true | all-gather | bytes 835584 | tf_op jit(solution)/shard_map/all_gather | solution.py:203
  53.0 1.5 %shard_map.121 = bf16[64,2,16,256]{3,2,1,0:T(8,128)(2,1)} custom-call(bf16[2,4,272,128]{3,2,1,0:T(8,128)(2,1)S(1)} %bitcast.43, bf16[256,512]{1,0:T(8,128)(2,1)S(1)} %bitcast.41), custom_call_target="tpu_custom_call" | custom-call | flops 268435456 | bytes 1048576 | tf_op jit(solution)/shard_map/pallas_call | solution.py:26
  54.4 7.4 %all-to-all-start.2 = ((bf16[16,4,32,256]{3,2,1,0:T(8,128)(2,1)}), bf16[16,4,32,256]{3,2,1,0:T(8,128)(2,1)S(1)}, u32[]{:S(2)}, u32[]{:S(2)}) async-start(bf16[16,4,32,256]{3,2,1,0:T(8,128)(2,1)} %bitcast.11), calls=%async_computation.2 | async-start | bytes 2097152 | tf_op jit(solution)/shard_map/all_to_all | solution.py:207
  62.6 2.6 %collective-permute-start = (bf16[4,256,128]{2,1,0:T(8,128)(2,1)S(1)}, bf16[4,256,128]{2,1,0:T(8,128)(2,1)S(1)}, u32[]{:S(2)}, u32[]{:S(2)}) collective-permute-start(bf16[4,256,128]{2,1,0:T(8,128)(2,1)S(1)} %get-tuple-element.22), channel_id=1, source_target_pairs={{0,1},{1,0},{2,3},{3,2},{4,5},{5,4},{6,7},{7,6},{8,9},{9,8},{10,11... | collective-permute-start | bytes 786440 | tf_op jit(solution)/shard_map/ppermute | solution.py:210
  65.2 1.1 collective-permute-done.other
  66.4 1.9 %collective-permute-start.1 = (bf16[256,128]{1,0:T(8,128)(2,1)S(1)}, bf16[256,128]{1,0:T(8,128)(2,1)S(1)}, u32[]{:S(2)}, u32[]{:S(2)}) collective-permute-start(bf16[256,128]{1,0:T(8,128)(2,1)S(1)} %get-tuple-element.24), channel_id=1, source_target_pairs={{0,2},{2,4},{4,6},{6,0},{1,3},{3,5},{5,7},{7,1},{8,10},{10,12},{12... | collective-permute-start | bytes 196616 | tf_op jit(solution)/shard_map/ppermute | solution.py:213
  69.1 6.4 %collective-permute-done.1.b = bf16[256,128]{1,0:T(8,128)(2,1)S(1)} collective-permute-done((bf16[256,128]{1,0:T(8,128)(2,1)S(1)}, bf16[256,128]{1,0:T(8,128)(2,1)S(1)}, u32[]{:S(2)}, u32[]{:S(2)}) %collective-permute-start.1) | collective-permute-done | bytes 65568 | tf_op jit(solution)/shard_map/ppermute | solution.py:213
  75.4 1.4 %all-to-all-done.2.parts = bf16[16,4,32,256]{3,2,1,0:T(8,128)(2,1)S(1)} async-done(((bf16[16,4,32,256]{3,2,1,0:T(8,128)(2,1)}), bf16[16,4,32,256]{3,2,1,0:T(8,128)(2,1)S(1)}, u32[]{:S(2)}, u32[]{:S(2)}) %all-to-all-start.2) | async-done | bytes 1048608 | tf_op jit(solution)/shard_map/all_to_all | solution.py:207
  77.7 7.6 %all-to-all-start.3 = ((bf16[16,32,256]{2,1,0:T(8,128)(2,1)}), bf16[16,32,256]{2,1,0:T(8,128)(2,1)S(1)}, u32[]{:S(2)}, u32[]{:S(2)}) async-start(bf16[16,32,256]{2,1,0:T(8,128)(2,1)} %bitcast.12), calls=%async_computation.3 | async-start | bytes 524288 | tf_op jit(solution)/shard_map/all_to_all | solution.py:219
  86.4 7.2 %collective-permute-start.3 = (bf16[256,128]{1,0:T(8,128)(2,1)S(1)}, bf16[256,128]{1,0:T(8,128)(2,1)S(1)}, u32[]{:S(2)}, u32[]{:S(2)}) collective-permute-start(bf16[256,128]{1,0:T(8,128)(2,1)S(1)} %get-tuple-element.26), channel_id=1, source_target_pairs={{0,6},{2,0},{4,2},{6,4},{1,7},{3,1},{5,3},{7,5},{8,14},{10,8},{12,... | collective-permute-start | bytes 196616 | tf_op jit(solution)/shard_map/ppermute | solution.py:213
  93.6 5.9 %all-to-all-done.3 = bf16[16,32,256]{2,1,0:T(8,128)(2,1)S(1)} async-done(((bf16[16,32,256]{2,1,0:T(8,128)(2,1)}), bf16[16,32,256]{2,1,0:T(8,128)(2,1)S(1)}, u32[]{:S(2)}, u32[]{:S(2)}) %all-to-all-start.3) | async-done | bytes 262176 | tf_op jit(solution)/shard_map/all_to_all | solution.py:219
  99.5 1.5 %shard_map.128 = f32[16,8,128]{2,1,0:T(8,128)} custom-call(bf16[128,256]{1,0:T(8,128)(2,1)S(1)} %bitcast.46, bf16[2048,256]{1,0:T(8,128)(2,1)S(1)} %bitcast.39), custom_call_target="tpu_custom_call" | custom-call | flops 268435456 | bytes 1048576 | tf_op jit(solution)/shard_map/pallas_call | solution.py:26
  100.9 8.6 %all-to-all-start.4 = ((f32[16,8,128]{2,1,0:T(8,128)}), f32[16,8,128]{2,1,0:T(8,128)S(1)}, u32[]{:S(2)}, u32[]{:S(2)}) async-start(f32[16,8,128]{2,1,0:T(8,128)} %shard_map.128), calls=%async_computation.4 | async-start | bytes 131072 | tf_op jit(solution)/shard_map/all_to_all | solution.py:233
  109.6 7.0 %collective-permute-start.2 = (bf16[256,128]{1,0:T(8,128)(2,1)S(1)}, bf16[256,128]{1,0:T(8,128)(2,1)S(1)}, u32[]{:S(2)}, u32[]{:S(2)}) collective-permute-start(bf16[256,128]{1,0:T(8,128)(2,1)S(1)} %get-tuple-element.25), channel_id=1, source_target_pairs={{0,4},{2,6},{4,0},{6,2},{1,5},{3,7},{5,1},{7,3},{8,12},{10,14},{12... | collective-permute-start | bytes 196616 | tf_op jit(solution)/shard_map/ppermute | solution.py:213
  117.3 14.4 %all-to-all-start.5 = ((f32[8,8,128]{2,1,0:T(8,128)}), f32[8,8,128]{2,1,0:T(8,128)S(1)}, u32[]{:S(2)}, u32[]{:S(2)}) async-start(f32[8,8,128]{2,1,0:T(8,128)} %shard_map.129), calls=%async_computation.5 | async-start | bytes 65536 | tf_op jit(solution)/shard_map/all_to_all | solution.py:236
  132.5 1.9 %all_gather.19.grads = bf16[256,256]{1,0:T(8,128)(2,1)S(1)} all-gather(bf16[128,256]{1,0:T(8,128)(2,1)S(1)} %bitcast.47), channel_id=1, replica_groups=mesh['x'=4,'y'=4,'l'=4,'h'=4,'c'=2] {'c'}, dimensions={0}, use_global_device_ids=true | all-gather | bytes 196608 | tf_op jit(solution)/shard_map/all_gather | solution.py:222
  134.4 1.9 %shard_map.127 = f32[2048,256]{1,0:T(8,128)} custom-call(bf16[128,16]{1,0:T(8,128)(2,1)S(1)} %copy.28.hidden_t, bf16[256,256]{1,0:T(8,128)(2,1)S(1)} %all_gather.19.grads), custom_call_target="tpu_custom_call" | custom-call | flops 268435456 | bytes 1048576 | tf_op jit(solution)/shard_map/pallas_call | solution.py:26
  136.6 0.9 shard_map.130
  (44 shorter events, 7.4 us)
Async XLA Ops:
  0.6 21.6 %copy-start.6 = (s32[16,2]{0,1:T(2,128)S(1)}, s32[16,2]{0,1:T(2,128)}, u32[]{:S(2)}) copy-start(s32[16,2]{0,1:T(2,128)} %param.11) | copy-start | bytes 388
  0.6 21.7 %copy-start.3 = (bf16[256,2,256]{2,1,0:T(2,128)(2,1)S(1)}, bf16[256,2,256]{2,1,0:T(2,128)(2,1)}, u32[]{:S(2)}) copy-start(bf16[256,2,256]{2,1,0:T(2,128)(2,1)} %param.9) | copy-start | bytes 786436
  3.3 11.0 %all-to-all-start = ((bf16[4,32,256]{2,1,0:T(8,128)(2,1)}), bf16[4,32,256]{2,1,0:T(8,128)(2,1)S(1)}, u32[]{:S(2)}, u32[]{:S(2)}) async-start(bf16[4,32,256]{2,1,0:T(8,128)(2,1)} %shard_map.120), calls=%async_computation | async-start | bytes 131072 | tf_op jit(solution)/shard_map/all_to_all | solution.py:196
  15.4 39.0 %all-to-all-start.1 = ((bf16[16,128,256]{2,1,0:T(8,128)(2,1)}), bf16[16,128,256]{2,1,0:T(8,128)(2,1)S(1)}, u32[]{:S(2)}, u32[]{:S(2)}) async-start(bf16[16,128,256]{2,1,0:T(8,128)(2,1)} %broadcast_in_dim.5), calls=%async_computation.1 | async-start | bytes 2097152 | tf_op jit(solution)/shard_map/all_to_all | solution.py:179
  52.9 1.5 %copy-start.1 = (bf16[8,272,128]{2,1,0:T(8,128)(2,1)}, bf16[8,272,128]{2,1,0:T(8,128)(2,1)S(1)}, u32[]{:S(2)}) copy-start(bf16[8,272,128]{2,1,0:T(8,128)(2,1)S(1)} %all-gather.1) | copy-start | bytes 1671172
  54.4 22.4 %all-to-all-start.2 = ((bf16[16,4,32,256]{3,2,1,0:T(8,128)(2,1)}), bf16[16,4,32,256]{3,2,1,0:T(8,128)(2,1)S(1)}, u32[]{:S(2)}, u32[]{:S(2)}) async-start(bf16[16,4,32,256]{3,2,1,0:T(8,128)(2,1)} %bitcast.11), calls=%async_computation.2 | async-start | bytes 2097152 | tf_op jit(solution)/shard_map/all_to_all | solution.py:207
  61.9 23.7 %copy-start.5 = (f32[208]{0:T(256)S(1)}, f32[208]{0:T(256)}, u32[]{:S(2)}) copy-start(f32[208]{0:T(256)} %table.1) | copy-start | bytes 2500
  61.9 24.1 %copy-start.2 = (f32[128,128]{1,0:T(8,128)S(1)}, f32[128,128]{1,0:T(8,128)}, u32[]{:S(2)}) copy-start(f32[128,128]{1,0:T(8,128)} %first.1) | copy-start | bytes 196612
  61.9 24.3 %copy-start.4 = (f32[4,128]{1,0:T(4,128)S(1)}, f32[4,128]{1,0:T(4,128)}, u32[]{:S(2)}) copy-start(f32[4,128]{1,0:T(4,128)} %sensor.1) | copy-start | bytes 6148
  61.9 37.6 %copy-start = (bf16[128,16,256]{2,1,0:T(8,128)(2,1)S(1)}, bf16[128,16,256]{2,1,0:T(8,128)(2,1)}, u32[]{:S(2)}) copy-start(bf16[128,16,256]{2,1,0:T(8,128)(2,1)} %param.17) | copy-start | bytes 3145732
  62.6 3.7 %collective-permute-start = (bf16[4,256,128]{2,1,0:T(8,128)(2,1)S(1)}, bf16[4,256,128]{2,1,0:T(8,128)(2,1)S(1)}, u32[]{:S(2)}, u32[]{:S(2)}) collective-permute-start(bf16[4,256,128]{2,1,0:T(8,128)(2,1)S(1)} %get-tuple-element.22), channel_id=1, source_target_pairs={{0,1},{1,0},{2,3},{3,2},{4,5},{5,4},{6,7},{7,6},{8,9},{9,8},{10,11... | collective-permute-start | bytes 786440 | tf_op jit(solution)/shard_map/ppermute | solution.py:210
  66.4 9.0 %collective-permute-start.1 = (bf16[256,128]{1,0:T(8,128)(2,1)S(1)}, bf16[256,128]{1,0:T(8,128)(2,1)S(1)}, u32[]{:S(2)}, u32[]{:S(2)}) collective-permute-start(bf16[256,128]{1,0:T(8,128)(2,1)S(1)} %get-tuple-element.24), channel_id=1, source_target_pairs={{0,2},{2,4},{4,6},{6,0},{1,3},{3,5},{5,7},{7,1},{8,10},{10,12},{12... | collective-permute-start | bytes 196616 | tf_op jit(solution)/shard_map/ppermute | solution.py:213
  77.7 21.7 %all-to-all-start.3 = ((bf16[16,32,256]{2,1,0:T(8,128)(2,1)}), bf16[16,32,256]{2,1,0:T(8,128)(2,1)S(1)}, u32[]{:S(2)}, u32[]{:S(2)}) async-start(bf16[16,32,256]{2,1,0:T(8,128)(2,1)} %bitcast.12), calls=%async_computation.3 | async-start | bytes 524288 | tf_op jit(solution)/shard_map/all_to_all | solution.py:219
  86.4 30.2 %collective-permute-start.3 = (bf16[256,128]{1,0:T(8,128)(2,1)S(1)}, bf16[256,128]{1,0:T(8,128)(2,1)S(1)}, u32[]{:S(2)}, u32[]{:S(2)}) collective-permute-start(bf16[256,128]{1,0:T(8,128)(2,1)S(1)} %get-tuple-element.26), channel_id=1, source_target_pairs={{0,6},{2,0},{4,2},{6,4},{1,7},{3,1},{5,3},{7,5},{8,14},{10,8},{12,... | collective-permute-start | bytes 196616 | tf_op jit(solution)/shard_map/ppermute | solution.py:213
  100.9 15.7 %all-to-all-start.4 = ((f32[16,8,128]{2,1,0:T(8,128)}), f32[16,8,128]{2,1,0:T(8,128)S(1)}, u32[]{:S(2)}, u32[]{:S(2)}) async-start(f32[16,8,128]{2,1,0:T(8,128)} %shard_map.128), calls=%async_computation.4 | async-start | bytes 131072 | tf_op jit(solution)/shard_map/all_to_all | solution.py:233
  109.6 22.3 %collective-permute-start.2 = (bf16[256,128]{1,0:T(8,128)(2,1)S(1)}, bf16[256,128]{1,0:T(8,128)(2,1)S(1)}, u32[]{:S(2)}, u32[]{:S(2)}) collective-permute-start(bf16[256,128]{1,0:T(8,128)(2,1)S(1)} %get-tuple-element.25), channel_id=1, source_target_pairs={{0,4},{2,6},{4,0},{6,2},{1,5},{3,7},{5,1},{7,3},{8,12},{10,14},{12... | collective-permute-start | bytes 196616 | tf_op jit(solution)/shard_map/ppermute | solution.py:213
  117.3 19.4 %all-to-all-start.5 = ((f32[8,8,128]{2,1,0:T(8,128)}), f32[8,8,128]{2,1,0:T(8,128)S(1)}, u32[]{:S(2)}, u32[]{:S(2)}) async-start(f32[8,8,128]{2,1,0:T(8,128)} %shard_map.129), calls=%async_computation.5 | async-start | bytes 65536 | tf_op jit(solution)/shard_map/all_to_all | solution.py:236

commit v3 on v2

--- a/solution.py
+++ b/solution.py
@@ -107,9 +107,12 @@
         outs[step][...] = (keep[step].astype(F32) + other[step].astype(F32)).astype(BF)
 
 
-def join_body(a, b, c, d, out):
-    total = a[...].astype(F32) + b[...].astype(F32)
-    out[...] = (total + c[...].astype(F32) + d[...].astype(F32)).astype(BF)
+def add_body(a, b, out):
+    out[...] = (a[...].astype(F32) + b[...].astype(F32)).astype(BF)
+
+
+def join_body(a, b, c, out):
+    out[...] = (a[...].astype(F32) + b[...].astype(F32) + c[...].astype(F32)).astype(BF)
 
 
 def grad_body(cot, masked, out):
@@ -209,12 +212,13 @@
     keep, send = call(embed_body, [shape, shape], [VMEM, VMEM], masked, kernels, flops=2**28)
     other = lax.ppermute(send, "c", [(0, 1), (1, 0)])
     shares = call(pair_body, [((rows, 128), BF)] * H, [VMEM, VMEM], keep, other, flops=2**18)
-    shares = [shares[0]] + [
-        lax.ppermute(shares[step], "h", [(i, (i + step) % H) for i in range(H)]) for step in range(1, H)
-    ]
-    (embed,) = call(join_body, [((rows, 128), BF)], [VMEM] * H, *shares, flops=2**18)
-
-    grads, *_ = lax.optimization_barrier((grads, shares[1]))
+    up, down = [(i, (i + 1) % H) for i in range(H)], [(i, (i - 1) % H) for i in range(H)]
+    first = lax.ppermute(shares[2], "h", up)
+    third = lax.ppermute(shares[3], "h", down)
+    (second,) = call(add_body, [((rows, 128), BF)], [VMEM] * 2, shares[1], first, flops=2**16)
+    second = lax.ppermute(second, "h", up)
+
+    grads, *_ = lax.optimization_barrier((grads, first, third))
     (grads,) = call(sum_xy_body, [((L, H, BD * DS, P2), BF)], [VMEM], grads, flops=2**20)
     grads = lax.all_to_all(grads.reshape(L * H, BD * DS, P2), ("l", "h"), 0, 0, tiled=True)
     (grads,) = call(sum_l_body, [((H, BD * DS, P2), BF)], [VMEM], grads.reshape(L, H, BD * DS, P2), flops=2**18)
@@ -228,13 +232,15 @@
     hidden_t = jax.nn.silu(preact).astype(BF).T
     slope = silu_slope(preact)
 
+    (embed,) = call(join_body, [((rows, 128), BF)], [VMEM] * 3, shares[0], second, third, flops=2**18)
     bands = C * H * BD
     (parts,) = call(hidden_grad_body, [((X * Y, bands // C, HID), F32)], [VMEM, VMEM], mine, weight, flops=2**28)
     parts = lax.all_to_all(parts, ("x", "y"), 0, 0, tiled=True)
-    parts, *_ = lax.optimization_barrier((parts, shares[3]))
+    (grad_out,) = call(out_grad_body, [((HID * DS, P2), F32)], [VMEM, VMEM], hidden_t, grads, flops=2**28)
+    parts, *_ = lax.optimization_barrier((parts, grad_out))
+    parts, *_ = lax.optimization_barrier((parts, second))
     (parts,) = call(spread_body, [((L * C, bands // C, HID), F32)], [VMEM], parts, flops=2**16)
     parts = lax.all_to_all(parts, ("l", "c"), 0, 0, tiled=True).reshape(L, bands, HID)
-    (grad_out,) = call(out_grad_body, [((HID * DS, P2), F32)], [VMEM, VMEM], hidden_t, grads, flops=2**28)
     grad_first, grad_sensor = call(
         final_body, [(first_weight.shape, F32), (sensor_embed.shape, F32)], [VMEM] * 4,
         parts, slope, features, sensor_hot, flops=2**20,

time: 139 us -> 138 us (level)
  starting transfers between devices: 69.9 us -> 61 us
  blocking collectives: 32.1 us -> 38.6 us
  waiting for transfers between devices: 18.1 us -> 20 us
    all_gather x1, blocking collectives: 1.89 us -> 8.39 us  [local(): grads = lax.all_gather(mine, 'c', axis=0, tiled=True)]
    all_to_all x1, starting transfers between devices: 14.4 us -> 8.1 us  [local(): lax.all_to_all(parts, ('l', 'c'), 0, 0, tiled=True).reshape(L, bands, HID)]
    all_to_all x1, waiting for transfers between devices: 0.35 us -> 4.24 us  [local(): lax.all_to_all(parts, ('l', 'c'), 0, 0, tiled=True).reshape(L, bands, HID)]
    all_to_all x1, starting transfers between devices: 8.61 us -> 6.95 us  [local(): parts = lax.all_to_all(parts, ('x', 'y'), 0, 0, tiled=True)]
    all_to_all x1, waiting for transfers between devices: 1.43 us -> 0.01 us  [local(): lax.all_to_all(grads.reshape(X * Y, L, BD * DS, P2), ('x', 'y'), 0, 0, ti...]
    pallas_call x11 -> x12, Pallas kernels: 11.3 us -> 11.3 us  [call(): pl.pallas_call(body, out_shape=[jax.ShapeDtypeStruct(shape, dtype) for sh...]
  transfers between devices with their start and end apart: 10 -> 10, of which waited for: 6 -> 5; matrix products, arithmetic and copies ran while one was open for 3% -> 3% of each run, Pallas kernels for 5% -> 5%
where the time goes in v3:
time: 138 us; the launch traced here: 137 us
  starting transfers between devices  61 us (44%)
  blocking collectives  38.6 us (28%)
  waiting for transfers between devices  20 us (14%)
  Pallas kernels  11.3 us (8%)
  other arithmetic  3.1 us (2%)
  local copies, waits for them, and re-layouts  1.5 us (1%)
    all_gather x1, blocking collectives, local(): lax.all_gather(cot_own, 'h', axis=0, tiled=False)  23.3 us
    pallas_call x12, Pallas kernels, call(): pl.pallas_call(body, out_shape=[jax.ShapeDtypeStruct(shape, dtype) for sh...  11.3 us
    all_gather x1, blocking collectives, local(): grads = lax.all_gather(mine, 'c', axis=0, tiled=True)  8.39 us
    all_to_all x1, starting transfers between devices, local(): lax.all_to_all(parts, ('l', 'c'), 0, 0, tiled=True).reshape(L, bands, HID)  8.1 us
    all_to_all x1, starting transfers between devices, local(): lax.all_to_all(grads.reshape(X * Y, L, BD * DS, P2), ('x', 'y'), 0, 0, ti...  7.41 us
    ppermute x1, starting transfers between devices, local(): third = lax.ppermute(shares[3], 'h', down)  7.27 us
    ppermute x1, starting transfers between devices, local(): second = lax.ppermute(second, 'h', up)  7.18 us
    all_to_all x1, starting transfers between devices, local(): parts = lax.all_to_all(parts, ('x', 'y'), 0, 0, tiled=True)  6.95 us
  transfers between devices with their start and end apart: 10, of which 5 were waited for; matrix products, arithmetic and copies ran while one was open for 3% of the time, Pallas kernels for 5%

profile of v3, /device:TPU:1, one launch (start us, length us, event | category | flops | bytes accessed | tf_op | source)
XLA Modules:
  0.0 137.0 jit_solution(8943914294811906902)
XLA Ops:
  0.7 2.6 %shard_map.120 = bf16[4,32,256]{2,1,0:T(8,128)(2,1)} custom-call(s32[2]{0:T(128)} %idx.1, s32[2]{0:T(128)} %sens.1, f32[208]{0:T(256)} %table.1, f32[128,128]{1,0:T(8,128)} %first.1, f32[4,128]{1,0:T(4,128)} %sensor.1, bf16[2048,256]{1,0:T(8,128)(2,1)} %bitcast.38), custom_call_target="tpu_custom_call" | custom-call | flops 33554432 | bytes 1048576 | tf_op jit(solution)/shard_map/pallas_call | solution.py:26
  3.3 6.4 %all-to-all-start = ((bf16[4,32,256]{2,1,0:T(8,128)(2,1)}), bf16[4,32,256]{2,1,0:T(8,128)(2,1)S(1)}, u32[]{:S(2)}, u32[]{:S(2)}) async-start(bf16[4,32,256]{2,1,0:T(8,128)(2,1)} %shard_map.120), calls=%async_computation | async-start | bytes 131072 | tf_op jit(solution)/shard_map/all_to_all | solution.py:199
  11.3 3.0 %all-to-all-done = bf16[4,32,256]{2,1,0:T(8,128)(2,1)S(1)} async-done(((bf16[4,32,256]{2,1,0:T(8,128)(2,1)}), bf16[4,32,256]{2,1,0:T(8,128)(2,1)S(1)}, u32[]{:S(2)}, u32[]{:S(2)}) %all-to-all-start) | async-done | bytes 65568 | tf_op jit(solution)/shard_map/all_to_all | solution.py:199
  14.3 1.1 broadcast_in_dim.5
  15.4 6.8 %all-to-all-start.1 = ((bf16[16,128,256]{2,1,0:T(8,128)(2,1)}), bf16[16,128,256]{2,1,0:T(8,128)(2,1)S(1)}, u32[]{:S(2)}, u32[]{:S(2)}) async-start(bf16[16,128,256]{2,1,0:T(8,128)(2,1)} %broadcast_in_dim.5), calls=%async_computation.1 | async-start | bytes 2097152 | tf_op jit(solution)/shard_map/all_to_all | solution.py:182
  22.7 23.3 %all-gather = bf16[1088,128]{1,0:T(8,128)(2,1)S(1)} all-gather(bf16[272,128]{1,0:T(8,128)(2,1)S(1)} %pad_maximum_fusion), channel_id=2, replica_groups=mesh['x'=4,'y'=4,'l'=4,'h'=4,'c'=2] {'h'}, dimensions={0}, use_global_device_ids=true | all-gather | bytes 348160 | tf_op jit(solution)/shard_map/all_gather | solution.py:206
  46.1 6.9 %all-gather.1 = bf16[8,272,128]{2,1,0:T(8,128)(2,1)S(1)} all-gather(bf16[4,272,128]{2,1,0:T(8,128)(2,1)S(1)} %bitcast.50), channel_id=3, replica_groups=mesh['x'=4,'y'=4,'l'=4,'h'=4,'c'=2] {'c'}, dimensions={0}, use_global_device_ids=true | all-gather | bytes 835584 | tf_op jit(solution)/shard_map/all_gather | solution.py:206
  53.0 1.5 %shard_map.121 = bf16[64,2,16,256]{3,2,1,0:T(8,128)(2,1)} custom-call(bf16[2,4,272,128]{3,2,1,0:T(8,128)(2,1)S(1)} %bitcast.43, bf16[256,512]{1,0:T(8,128)(2,1)S(1)} %bitcast.41), custom_call_target="tpu_custom_call" | custom-call | flops 268435456 | bytes 1048576 | tf_op jit(solution)/shard_map/pallas_call | solution.py:26
  54.4 7.4 %all-to-all-start.2 = ((bf16[16,4,32,256]{3,2,1,0:T(8,128)(2,1)}), bf16[16,4,32,256]{3,2,1,0:T(8,128)(2,1)S(1)}, u32[]{:S(2)}, u32[]{:S(2)}) async-start(bf16[16,4,32,256]{3,2,1,0:T(8,128)(2,1)} %bitcast.11), calls=%async_computation.2 | async-start | bytes 2097152 | tf_op jit(solution)/shard_map/all_to_all | solution.py:210
  62.6 2.6 %collective-permute-start = (bf16[4,256,128]{2,1,0:T(8,128)(2,1)S(1)}, bf16[4,256,128]{2,1,0:T(8,128)(2,1)S(1)}, u32[]{:S(2)}, u32[]{:S(2)}) collective-permute-start(bf16[4,256,128]{2,1,0:T(8,128)(2,1)S(1)} %get-tuple-element.23), channel_id=1, source_target_pairs={{0,1},{1,0},{2,3},{3,2},{4,5},{5,4},{6,7},{7,6},{8,9},{9,8},{10,11... | collective-permute-start | bytes 786440 | tf_op jit(solution)/shard_map/ppermute | solution.py:213
  65.2 1.1 collective-permute-done.other
  66.4 1.9 %collective-permute-start.1 = (bf16[256,128]{1,0:T(8,128)(2,1)S(1)}, bf16[256,128]{1,0:T(8,128)(2,1)S(1)}, u32[]{:S(2)}, u32[]{:S(2)}) collective-permute-start(bf16[256,128]{1,0:T(8,128)(2,1)S(1)} %get-tuple-element.26), channel_id=1, source_target_pairs={{0,2},{2,4},{4,6},{6,0},{1,3},{3,5},{5,7},{7,1},{8,10},{10,12},{12... | collective-permute-start | bytes 196616 | tf_op jit(solution)/shard_map/ppermute | solution.py:216
  68.3 7.3 %collective-permute-start.3 = (bf16[256,128]{1,0:T(8,128)(2,1)S(1)}, bf16[256,128]{1,0:T(8,128)(2,1)S(1)}, u32[]{:S(2)}, u32[]{:S(2)}) collective-permute-start(bf16[256,128]{1,0:T(8,128)(2,1)S(1)} %get-tuple-element.27), channel_id=1, source_target_pairs={{0,6},{2,0},{4,2},{6,4},{1,7},{3,1},{5,3},{7,5},{8,14},{10,8},{12,... | collective-permute-start | bytes 196616 | tf_op jit(solution)/shard_map/ppermute | solution.py:217
  76.3 5.5 %collective-permute-done.3.c = bf16[256,128]{1,0:T(8,128)(2,1)S(1)} collective-permute-done((bf16[256,128]{1,0:T(8,128)(2,1)S(1)}, bf16[256,128]{1,0:T(8,128)(2,1)S(1)}, u32[]{:S(2)}, u32[]{:S(2)}) %collective-permute-start.3) | collective-permute-done | bytes 65568 | tf_op jit(solution)/shard_map/ppermute | solution.py:217
  82.7 6.5 %all-to-all-start.3 = ((bf16[16,32,256]{2,1,0:T(8,128)(2,1)}), bf16[16,32,256]{2,1,0:T(8,128)(2,1)S(1)}, u32[]{:S(2)}, u32[]{:S(2)}) async-start(bf16[16,32,256]{2,1,0:T(8,128)(2,1)} %bitcast.12), calls=%async_computation.3 | async-start | bytes 524288 | tf_op jit(solution)/shard_map/all_to_all | solution.py:223
  90.2 7.2 %collective-permute-start.2 = (bf16[256,128]{1,0:T(8,128)(2,1)S(1)}, bf16[256,128]{1,0:T(8,128)(2,1)S(1)}, u32[]{:S(2)}, u32[]{:S(2)}) collective-permute-start(bf16[256,128]{1,0:T(8,128)(2,1)S(1)} %shard_map.124), channel_id=1, source_target_pairs={{0,2},{2,4},{4,6},{6,0},{1,3},{3,5},{5,7},{7,1},{8,10},{10,12},{12... | collective-permute-start | bytes 196616 | tf_op jit(solution)/shard_map/ppermute | solution.py:219
  97.4 6.2 %all-to-all-done.3 = bf16[16,32,256]{2,1,0:T(8,128)(2,1)S(1)} async-done(((bf16[16,32,256]{2,1,0:T(8,128)(2,1)}), bf16[16,32,256]{2,1,0:T(8,128)(2,1)S(1)}, u32[]{:S(2)}, u32[]{:S(2)}) %all-to-all-start.3) | async-done | bytes 262176 | tf_op jit(solution)/shard_map/all_to_all | solution.py:223
  103.6 1.5 %shard_map.129 = f32[16,8,128]{2,1,0:T(8,128)} custom-call(bf16[128,256]{1,0:T(8,128)(2,1)S(1)} %bitcast.46, bf16[2048,256]{1,0:T(8,128)(2,1)S(1)} %bitcast.39), custom_call_target="tpu_custom_call" | custom-call | flops 268435456 | bytes 1048576 | tf_op jit(solution)/shard_map/pallas_call | solution.py:26
  105.1 6.9 %all-to-all-start.4 = ((f32[16,8,128]{2,1,0:T(8,128)}), f32[16,8,128]{2,1,0:T(8,128)S(1)}, u32[]{:S(2)}, u32[]{:S(2)}) async-start(f32[16,8,128]{2,1,0:T(8,128)} %shard_map.129), calls=%async_computation.4 | async-start | bytes 131072 | tf_op jit(solution)/shard_map/all_to_all | solution.py:238
  112.2 8.4 %all_gather.19.grads = bf16[256,256]{1,0:T(8,128)(2,1)S(1)} all-gather(bf16[128,256]{1,0:T(8,128)(2,1)S(1)} %bitcast.47), channel_id=1, replica_groups=mesh['x'=4,'y'=4,'l'=4,'h'=4,'c'=2] {'c'}, dimensions={0}, use_global_device_ids=true | all-gather | bytes 196608 | tf_op jit(solution)/shard_map/all_gather | solution.py:226
  120.6 1.9 %shard_map.128 = f32[2048,256]{1,0:T(8,128)} custom-call(bf16[128,16]{1,0:T(8,128)(2,1)S(1)} %copy.28.hidden_t, bf16[256,256]{1,0:T(8,128)(2,1)S(1)} %all_gather.19.grads), custom_call_target="tpu_custom_call" | custom-call | flops 268435456 | bytes 1048576 | tf_op jit(solution)/shard_map/pallas_call | solution.py:26
  123.1 8.1 %all-to-all-start.5 = ((f32[8,8,128]{2,1,0:T(8,128)}), f32[8,8,128]{2,1,0:T(8,128)S(1)}, u32[]{:S(2)}, u32[]{:S(2)}) async-start(f32[8,8,128]{2,1,0:T(8,128)} %shard_map.130), calls=%async_computation.5 | async-start | bytes 65536 | tf_op jit(solution)/shard_map/all_to_all | solution.py:243
  131.9 4.2 %all-to-all-done.5 = f32[8,8,128]{2,1,0:T(8,128)S(1)} async-done(((f32[8,8,128]{2,1,0:T(8,128)}), f32[8,8,128]{2,1,0:T(8,128)S(1)}, u32[]{:S(2)}, u32[]{:S(2)}) %all-to-all-start.5) | async-done | bytes 32800 | tf_op jit(solution)/shard_map/all_to_all | solution.py:243
  136.1 0.9 shard_map.131
  (45 shorter events, 7.1 us)
Async XLA Ops:
  0.6 21.6 %copy-start.6 = (s32[16,2]{0,1:T(2,128)S(1)}, s32[16,2]{0,1:T(2,128)}, u32[]{:S(2)}) copy-start(s32[16,2]{0,1:T(2,128)} %param.11) | copy-start | bytes 388
  0.6 21.7 %copy-start.3 = (bf16[256,2,256]{2,1,0:T(2,128)(2,1)S(1)}, bf16[256,2,256]{2,1,0:T(2,128)(2,1)}, u32[]{:S(2)}) copy-start(bf16[256,2,256]{2,1,0:T(2,128)(2,1)} %param.9) | copy-start | bytes 786436
  3.3 11.0 %all-to-all-start = ((bf16[4,32,256]{2,1,0:T(8,128)(2,1)}), bf16[4,32,256]{2,1,0:T(8,128)(2,1)S(1)}, u32[]{:S(2)}, u32[]{:S(2)}) async-start(bf16[4,32,256]{2,1,0:T(8,128)(2,1)} %shard_map.120), calls=%async_computation | async-start | bytes 131072 | tf_op jit(solution)/shard_map/all_to_all | solution.py:199
  15.4 39.0 %all-to-all-start.1 = ((bf16[16,128,256]{2,1,0:T(8,128)(2,1)}), bf16[16,128,256]{2,1,0:T(8,128)(2,1)S(1)}, u32[]{:S(2)}, u32[]{:S(2)}) async-start(bf16[16,128,256]{2,1,0:T(8,128)(2,1)} %broadcast_in_dim.5), calls=%async_computation.1 | async-start | bytes 2097152 | tf_op jit(solution)/shard_map/all_to_all | solution.py:182
  52.9 1.5 %copy-start.1 = (bf16[8,272,128]{2,1,0:T(8,128)(2,1)}, bf16[8,272,128]{2,1,0:T(8,128)(2,1)S(1)}, u32[]{:S(2)}) copy-start(bf16[8,272,128]{2,1,0:T(8,128)(2,1)S(1)} %all-gather.1) | copy-start | bytes 1671172
  54.4 27.4 %all-to-all-start.2 = ((bf16[16,4,32,256]{3,2,1,0:T(8,128)(2,1)}), bf16[16,4,32,256]{3,2,1,0:T(8,128)(2,1)S(1)}, u32[]{:S(2)}, u32[]{:S(2)}) async-start(bf16[16,4,32,256]{3,2,1,0:T(8,128)(2,1)} %bitcast.11), calls=%async_computation.2 | async-start | bytes 2097152 | tf_op jit(solution)/shard_map/all_to_all | solution.py:210
  61.9 27.5 %copy-start.5 = (f32[208]{0:T(256)S(1)}, f32[208]{0:T(256)}, u32[]{:S(2)}) copy-start(f32[208]{0:T(256)} %table.1) | copy-start | bytes 2500
  61.9 27.9 %copy-start.2 = (f32[128,128]{1,0:T(8,128)S(1)}, f32[128,128]{1,0:T(8,128)}, u32[]{:S(2)}) copy-start(f32[128,128]{1,0:T(8,128)} %first.1) | copy-start | bytes 196612
  61.9 28.1 %copy-start.4 = (f32[4,128]{1,0:T(4,128)S(1)}, f32[4,128]{1,0:T(4,128)}, u32[]{:S(2)}) copy-start(f32[4,128]{1,0:T(4,128)} %sensor.1) | copy-start | bytes 6148
  61.9 41.7 %copy-start = (bf16[128,16,256]{2,1,0:T(8,128)(2,1)S(1)}, bf16[128,16,256]{2,1,0:T(8,128)(2,1)}, u32[]{:S(2)}) copy-start(bf16[128,16,256]{2,1,0:T(8,128)(2,1)} %param.17) | copy-start | bytes 3145732
  62.6 3.7 %collective-permute-start = (bf16[4,256,128]{2,1,0:T(8,128)(2,1)S(1)}, bf16[4,256,128]{2,1,0:T(8,128)(2,1)S(1)}, u32[]{:S(2)}, u32[]{:S(2)}) collective-permute-start(bf16[4,256,128]{2,1,0:T(8,128)(2,1)S(1)} %get-tuple-element.23), channel_id=1, source_target_pairs={{0,1},{1,0},{2,3},{3,2},{4,5},{5,4},{6,7},{7,6},{8,9},{9,8},{10,11... | collective-permute-start | bytes 786440 | tf_op jit(solution)/shard_map/ppermute | solution.py:213
  66.4 9.9 %collective-permute-start.1 = (bf16[256,128]{1,0:T(8,128)(2,1)S(1)}, bf16[256,128]{1,0:T(8,128)(2,1)S(1)}, u32[]{:S(2)}, u32[]{:S(2)}) collective-permute-start(bf16[256,128]{1,0:T(8,128)(2,1)S(1)} %get-tuple-element.26), channel_id=1, source_target_pairs={{0,2},{2,4},{4,6},{6,0},{1,3},{3,5},{5,7},{7,1},{8,10},{10,12},{12... | collective-permute-start | bytes 196616 | tf_op jit(solution)/shard_map/ppermute | solution.py:216
  68.3 13.5 %collective-permute-start.3 = (bf16[256,128]{1,0:T(8,128)(2,1)S(1)}, bf16[256,128]{1,0:T(8,128)(2,1)S(1)}, u32[]{:S(2)}, u32[]{:S(2)}) collective-permute-start(bf16[256,128]{1,0:T(8,128)(2,1)S(1)} %get-tuple-element.27), channel_id=1, source_target_pairs={{0,6},{2,0},{4,2},{6,4},{1,7},{3,1},{5,3},{7,5},{8,14},{10,8},{12,... | collective-permute-start | bytes 196616 | tf_op jit(solution)/shard_map/ppermute | solution.py:217
  82.7 20.9 %all-to-all-start.3 = ((bf16[16,32,256]{2,1,0:T(8,128)(2,1)}), bf16[16,32,256]{2,1,0:T(8,128)(2,1)S(1)}, u32[]{:S(2)}, u32[]{:S(2)}) async-start(bf16[16,32,256]{2,1,0:T(8,128)(2,1)} %bitcast.12), calls=%async_computation.3 | async-start | bytes 524288 | tf_op jit(solution)/shard_map/all_to_all | solution.py:223
  90.2 32.2 %collective-permute-start.2 = (bf16[256,128]{1,0:T(8,128)(2,1)S(1)}, bf16[256,128]{1,0:T(8,128)(2,1)S(1)}, u32[]{:S(2)}, u32[]{:S(2)}) collective-permute-start(bf16[256,128]{1,0:T(8,128)(2,1)S(1)} %shard_map.124), channel_id=1, source_target_pairs={{0,2},{2,4},{4,6},{6,0},{1,3},{3,5},{5,7},{7,1},{8,10},{10,12},{12... | collective-permute-start | bytes 196616 | tf_op jit(solution)/shard_map/ppermute | solution.py:219
  105.1 17.4 %all-to-all-start.4 = ((f32[16,8,128]{2,1,0:T(8,128)}), f32[16,8,128]{2,1,0:T(8,128)S(1)}, u32[]{:S(2)}, u32[]{:S(2)}) async-start(f32[16,8,128]{2,1,0:T(8,128)} %shard_map.129), calls=%async_computation.4 | async-start | bytes 131072 | tf_op jit(solution)/shard_map/all_to_all | solution.py:238
  123.1 13.1 %all-to-all-start.5 = ((f32[8,8,128]{2,1,0:T(8,128)}), f32[8,8,128]{2,1,0:T(8,128)S(1)}, u32[]{:S(2)}, u32[]{:S(2)}) async-start(f32[8,8,128]{2,1,0:T(8,128)} %shard_map.130), calls=%async_computation.5 | async-start | bytes 65536 | tf_op jit(solution)/shard_map/all_to_all | solution.py:243

commit v4 on v3

--- a/solution.py
+++ b/solution.py
@@ -117,7 +117,7 @@
 
 def grad_body(cot, masked, out):
     for b in range(H * C):
-        block = cot[b % C, b // C, 0:256, :]
+        block = cot[b // C, b % C, 0:256, :]
         part = lax.dot_general(block, masked[...], (((0,), (0,)), ((), ())), preferred_element_type=F32).astype(BF)
         for c in range(BD):
             out[8 * b : 8 * b + 8, c] = part[:, c * P2 : (c + 1) * P2].reshape(8, DS, P2)
@@ -203,7 +203,7 @@
     cot_own = jnp.concatenate([cotangent, tail], axis=0)
     cot_own, part_l = lax.optimization_barrier((cot_own, part_l))
     kernels = gather(part_l.reshape(L * BD * DS, P2), ("x", "y"), X * Y).reshape(X * Y * L, BD, DS, P2)
-    cot = lax.all_gather(lax.all_gather(cot_own, "h", axis=0, tiled=False), "c", axis=0, tiled=False)
+    cot = lax.all_gather(cot_own, ("h", "c"), axis=0, tiled=False).reshape(H, C, rows + 16, 128)
     (grads,) = call(grad_body, [((X * Y * L, BD, DS, P2), BF)], [VMEM, VMEM], cot, masked, flops=2**28)
 
     grads, kernels = lax.optimization_barrier((grads, kernels))
@@ -225,7 +225,7 @@
     mine = grads.reshape(H * BD * DS, P2)
     grads = lax.all_gather(mine, "c", axis=0, tiled=True)
 
-    every = cot[:, :, rows, : 2 * BD].astype(jnp.int32).reshape(C * H, 2 * BD)
+    every = cot[:, :, rows, : 2 * BD].astype(jnp.int32).swapaxes(0, 1).reshape(C * H, 2 * BD)
     features, sensor_hot, preact = hypernet(
         every[:, :BD].reshape(-1), every[:, BD:].reshape(-1), wave_table, first_weight, sensor_embed
     )

time: 138 us -> 137 us (level)
    all_gather x2 -> x1, blocking collectives: 30.2 us -> 29.2 us  [local(): lax.all_gather(cot_own, ('h', 'c'), axis=0, tiled=False)]
where the time goes in v4:
time: 137 us; the launch traced here: 136 us
  starting transfers between devices  60.6 us (44%)
  blocking collectives  37.6 us (27%)
  waiting for transfers between devices  19.9 us (15%)
  Pallas kernels  11.3 us (8%)
  other arithmetic  3.1 us (2%)
  local copies, waits for them, and re-layouts  1.78 us (1%)
    all_gather x1, blocking collectives, local(): lax.all_gather(cot_own, ('h', 'c'), axis=0, tiled=False)  29.2 us
    pallas_call x12, Pallas kernels, call(): pl.pallas_call(body, out_shape=[jax.ShapeDtypeStruct(shape, dtype) for sh...  11.3 us
    all_gather x1, blocking collectives, local(): grads = lax.all_gather(mine, 'c', axis=0, tiled=True)  8.41 us
    all_to_all x1, starting transfers between devices, local(): lax.all_to_all(parts, ('l', 'c'), 0, 0, tiled=True).reshape(L, bands, HID)  8.07 us
    all_to_all x1, starting transfers between devices, local(): lax.all_to_all(grads.reshape(X * Y, L, BD * DS, P2), ('x', 'y'), 0, 0, ti...  7.35 us
    ppermute x1, starting transfers between devices, local(): third = lax.ppermute(shares[3], 'h', down)  7.27 us
    ppermute x1, starting transfers between devices, local(): second = lax.ppermute(second, 'h', up)  7.18 us
    all_to_all x1, starting transfers between devices, local(): parts = lax.all_to_all(parts, ('x', 'y'), 0, 0, tiled=True)  6.93 us
  transfers between devices with their start and end apart: 10, of which 5 were waited for; matrix products, arithmetic and copies ran while one was open for 3% of the time, Pallas kernels for 5%

profile of v4, /device:TPU:1, one launch (start us, length us, event | category | flops | bytes accessed | tf_op | source)
XLA Modules:
  0.0 135.7 jit_solution(17840482629555617709)
XLA Ops:
  0.7 2.6 %shard_map.120 = bf16[4,32,256]{2,1,0:T(8,128)(2,1)} custom-call(s32[2]{0:T(128)} %idx.1, s32[2]{0:T(128)} %sens.1, f32[208]{0:T(256)} %table.1, f32[128,128]{1,0:T(8,128)} %first.1, f32[4,128]{1,0:T(4,128)} %sensor.1, bf16[2048,256]{1,0:T(8,128)(2,1)} %bitcast.41), custom_call_target="tpu_custom_call" | custom-call | flops 33554432 | bytes 1048576 | tf_op jit(solution)/shard_map/pallas_call | solution.py:26
  3.3 6.4 %all-to-all-start = ((bf16[4,32,256]{2,1,0:T(8,128)(2,1)}), bf16[4,32,256]{2,1,0:T(8,128)(2,1)S(1)}, u32[]{:S(2)}, u32[]{:S(2)}) async-start(bf16[4,32,256]{2,1,0:T(8,128)(2,1)} %shard_map.120), calls=%async_computation | async-start | bytes 131072 | tf_op jit(solution)/shard_map/all_to_all | solution.py:199
  10.5 0.8 pad_maximum_fusion
  11.3 3.0 %all-to-all-done = bf16[4,32,256]{2,1,0:T(8,128)(2,1)S(1)} async-done(((bf16[4,32,256]{2,1,0:T(8,128)(2,1)}), bf16[4,32,256]{2,1,0:T(8,128)(2,1)S(1)}, u32[]{:S(2)}, u32[]{:S(2)}) %all-to-all-start) | async-done | bytes 65568 | tf_op jit(solution)/shard_map/all_to_all | solution.py:199
  14.3 1.1 broadcast_in_dim.5
  15.4 6.8 %all-to-all-start.1 = ((bf16[16,128,256]{2,1,0:T(8,128)(2,1)}), bf16[16,128,256]{2,1,0:T(8,128)(2,1)S(1)}, u32[]{:S(2)}, u32[]{:S(2)}) async-start(bf16[16,128,256]{2,1,0:T(8,128)(2,1)} %broadcast_in_dim.5), calls=%async_computation.1 | async-start | bytes 2097152 | tf_op jit(solution)/shard_map/all_to_all | solution.py:182
  22.7 29.2 %all-gather = bf16[2176,128]{1,0:T(8,128)(2,1)S(1)} all-gather(bf16[272,128]{1,0:T(8,128)(2,1)S(1)} %pad_maximum_fusion), channel_id=2, replica_groups=mesh['x'=4,'y'=4,'l'=4,'h'=4,'c'=2] {'h','c'}, dimensions={0}, use_global_device_ids=true | all-gather | bytes 626688 | tf_op jit(solution)/shard_map/all_gather | solution.py:206
  51.9 1.5 %shard_map.121 = bf16[64,2,16,256]{3,2,1,0:T(8,128)(2,1)} custom-call(bf16[4,2,272,128]{3,2,1,0:T(8,128)(2,1)S(1)} %bitcast.46, bf16[256,512]{1,0:T(8,128)(2,1)S(1)} %bitcast.44), custom_call_target="tpu_custom_call" | custom-call | flops 268435456 | bytes 1048576 | tf_op jit(solution)/shard_map/pallas_call | solution.py:26
  53.4 7.4 %all-to-all-start.2 = ((bf16[16,4,32,256]{3,2,1,0:T(8,128)(2,1)}), bf16[16,4,32,256]{3,2,1,0:T(8,128)(2,1)S(1)}, u32[]{:S(2)}, u32[]{:S(2)}) async-start(bf16[16,4,32,256]{3,2,1,0:T(8,128)(2,1)} %bitcast.11), calls=%async_computation.2 | async-start | bytes 2097152 | tf_op jit(solution)/shard_map/all_to_all | solution.py:210
  61.5 2.4 %collective-permute-start = (bf16[4,256,128]{2,1,0:T(8,128)(2,1)S(1)}, bf16[4,256,128]{2,1,0:T(8,128)(2,1)S(1)}, u32[]{:S(2)}, u32[]{:S(2)}) collective-permute-start(bf16[4,256,128]{2,1,0:T(8,128)(2,1)S(1)} %get-tuple-element.23), channel_id=1, source_target_pairs={{0,1},{1,0},{2,3},{3,2},{4,5},{5,4},{6,7},{7,6},{8,9},{9,8},{10,11... | collective-permute-start | bytes 786440 | tf_op jit(solution)/shard_map/ppermute | solution.py:213
  63.9 1.1 collective-permute-done.other
  65.1 1.9 %collective-permute-start.1 = (bf16[256,128]{1,0:T(8,128)(2,1)S(1)}, bf16[256,128]{1,0:T(8,128)(2,1)S(1)}, u32[]{:S(2)}, u32[]{:S(2)}) collective-permute-start(bf16[256,128]{1,0:T(8,128)(2,1)S(1)} %get-tuple-element.26), channel_id=1, source_target_pairs={{0,2},{2,4},{4,6},{6,0},{1,3},{3,5},{5,7},{7,1},{8,10},{10,12},{12... | collective-permute-start | bytes 196616 | tf_op jit(solution)/shard_map/ppermute | solution.py:216
  67.0 7.3 %collective-permute-start.3 = (bf16[256,128]{1,0:T(8,128)(2,1)S(1)}, bf16[256,128]{1,0:T(8,128)(2,1)S(1)}, u32[]{:S(2)}, u32[]{:S(2)}) collective-permute-start(bf16[256,128]{1,0:T(8,128)(2,1)S(1)} %get-tuple-element.27), channel_id=1, source_target_pairs={{0,6},{2,0},{4,2},{6,4},{1,7},{3,1},{5,3},{7,5},{8,14},{10,8},{12,... | collective-permute-start | bytes 196616 | tf_op jit(solution)/shard_map/ppermute | solution.py:217
  75.2 5.4 %collective-permute-done.3.c = bf16[256,128]{1,0:T(8,128)(2,1)S(1)} collective-permute-done((bf16[256,128]{1,0:T(8,128)(2,1)S(1)}, bf16[256,128]{1,0:T(8,128)(2,1)S(1)}, u32[]{:S(2)}, u32[]{:S(2)}) %collective-permute-start.3) | collective-permute-done | bytes 65568 | tf_op jit(solution)/shard_map/ppermute | solution.py:217
  81.5 6.4 %all-to-all-start.3 = ((bf16[16,32,256]{2,1,0:T(8,128)(2,1)}), bf16[16,32,256]{2,1,0:T(8,128)(2,1)S(1)}, u32[]{:S(2)}, u32[]{:S(2)}) async-start(bf16[16,32,256]{2,1,0:T(8,128)(2,1)} %bitcast.12), calls=%async_computation.3 | async-start | bytes 524288 | tf_op jit(solution)/shard_map/all_to_all | solution.py:223
  89.0 7.2 %collective-permute-start.2 = (bf16[256,128]{1,0:T(8,128)(2,1)S(1)}, bf16[256,128]{1,0:T(8,128)(2,1)S(1)}, u32[]{:S(2)}, u32[]{:S(2)}) collective-permute-start(bf16[256,128]{1,0:T(8,128)(2,1)S(1)} %shard_map.124), channel_id=1, source_target_pairs={{0,2},{2,4},{4,6},{6,0},{1,3},{3,5},{5,7},{7,1},{8,10},{10,12},{12... | collective-permute-start | bytes 196616 | tf_op jit(solution)/shard_map/ppermute | solution.py:219
  96.2 6.1 %all-to-all-done.3 = bf16[16,32,256]{2,1,0:T(8,128)(2,1)S(1)} async-done(((bf16[16,32,256]{2,1,0:T(8,128)(2,1)}), bf16[16,32,256]{2,1,0:T(8,128)(2,1)S(1)}, u32[]{:S(2)}, u32[]{:S(2)}) %all-to-all-start.3) | async-done | bytes 262176 | tf_op jit(solution)/shard_map/all_to_all | solution.py:223
  102.3 1.5 %shard_map.129 = f32[16,8,128]{2,1,0:T(8,128)} custom-call(bf16[128,256]{1,0:T(8,128)(2,1)S(1)} %bitcast.49, bf16[2048,256]{1,0:T(8,128)(2,1)S(1)} %bitcast.42), custom_call_target="tpu_custom_call" | custom-call | flops 268435456 | bytes 1048576 | tf_op jit(solution)/shard_map/pallas_call | solution.py:26
  103.8 6.9 %all-to-all-start.4 = ((f32[16,8,128]{2,1,0:T(8,128)}), f32[16,8,128]{2,1,0:T(8,128)S(1)}, u32[]{:S(2)}, u32[]{:S(2)}) async-start(f32[16,8,128]{2,1,0:T(8,128)} %shard_map.129), calls=%async_computation.4 | async-start | bytes 131072 | tf_op jit(solution)/shard_map/all_to_all | solution.py:238
  110.9 8.4 %all_gather.11.grads = bf16[256,256]{1,0:T(8,128)(2,1)S(1)} all-gather(bf16[128,256]{1,0:T(8,128)(2,1)S(1)} %bitcast.50), channel_id=1, replica_groups=mesh['x'=4,'y'=4,'l'=4,'h'=4,'c'=2] {'c'}, dimensions={0}, use_global_device_ids=true | all-gather | bytes 196608 | tf_op jit(solution)/shard_map/all_gather | solution.py:226
  119.3 1.9 %shard_map.128 = f32[2048,256]{1,0:T(8,128)} custom-call(bf16[128,16]{1,0:T(8,128)(2,1)S(1)} %copy.20.hidden_t, bf16[256,256]{1,0:T(8,128)(2,1)S(1)} %all_gather.11.grads), custom_call_target="tpu_custom_call" | custom-call | flops 268435456 | bytes 1048576 | tf_op jit(solution)/shard_map/pallas_call | solution.py:26
  121.8 8.1 %all-to-all-start.5 = ((f32[8,8,128]{2,1,0:T(8,128)}), f32[8,8,128]{2,1,0:T(8,128)S(1)}, u32[]{:S(2)}, u32[]{:S(2)}) async-start(f32[8,8,128]{2,1,0:T(8,128)} %shard_map.130), calls=%async_computation.5 | async-start | bytes 65536 | tf_op jit(solution)/shard_map/all_to_all | solution.py:243
  130.6 4.2 %all-to-all-done.5 = f32[8,8,128]{2,1,0:T(8,128)S(1)} async-done(((f32[8,8,128]{2,1,0:T(8,128)}), f32[8,8,128]{2,1,0:T(8,128)S(1)}, u32[]{:S(2)}, u32[]{:S(2)}) %all-to-all-start.5) | async-done | bytes 32800 | tf_op jit(solution)/shard_map/all_to_all | solution.py:243
  134.8 0.9 shard_map.131
  (48 shorter events, 6.5 us)
Async XLA Ops:
  0.6 21.6 %copy-start.6 = (s32[16,2]{0,1:T(2,128)S(1)}, s32[16,2]{0,1:T(2,128)}, u32[]{:S(2)}) copy-start(s32[16,2]{0,1:T(2,128)} %param.11) | copy-start | bytes 388
  0.6 21.7 %copy-start.3 = (bf16[256,2,256]{2,1,0:T(2,128)(2,1)S(1)}, bf16[256,2,256]{2,1,0:T(2,128)(2,1)}, u32[]{:S(2)}) copy-start(bf16[256,2,256]{2,1,0:T(2,128)(2,1)} %param.9) | copy-start | bytes 786436
  3.3 11.0 %all-to-all-start = ((bf16[4,32,256]{2,1,0:T(8,128)(2,1)}), bf16[4,32,256]{2,1,0:T(8,128)(2,1)S(1)}, u32[]{:S(2)}, u32[]{:S(2)}) async-start(bf16[4,32,256]{2,1,0:T(8,128)(2,1)} %shard_map.120), calls=%async_computation | async-start | bytes 131072 | tf_op jit(solution)/shard_map/all_to_all | solution.py:199
  15.4 38.0 %all-to-all-start.1 = ((bf16[16,128,256]{2,1,0:T(8,128)(2,1)}), bf16[16,128,256]{2,1,0:T(8,128)(2,1)S(1)}, u32[]{:S(2)}, u32[]{:S(2)}) async-start(bf16[16,128,256]{2,1,0:T(8,128)(2,1)} %broadcast_in_dim.5), calls=%async_computation.1 | async-start | bytes 2097152 | tf_op jit(solution)/shard_map/all_to_all | solution.py:182
  51.9 1.5 %copy-start.1 = (bf16[2176,128]{1,0:T(8,128)(2,1)}, bf16[2176,128]{1,0:T(8,128)(2,1)S(1)}, u32[]{:S(2)}) copy-start(bf16[2176,128]{1,0:T(8,128)(2,1)S(1)} %all-gather) | copy-start | bytes 1671172
  53.4 27.2 %all-to-all-start.2 = ((bf16[16,4,32,256]{3,2,1,0:T(8,128)(2,1)}), bf16[16,4,32,256]{3,2,1,0:T(8,128)(2,1)S(1)}, u32[]{:S(2)}, u32[]{:S(2)}) async-start(bf16[16,4,32,256]{3,2,1,0:T(8,128)(2,1)} %bitcast.11), calls=%async_computation.2 | async-start | bytes 2097152 | tf_op jit(solution)/shard_map/all_to_all | solution.py:210
  60.7 27.4 %copy-start.5 = (f32[208]{0:T(256)S(1)}, f32[208]{0:T(256)}, u32[]{:S(2)}) copy-start(f32[208]{0:T(256)} %table.1) | copy-start | bytes 2500
  60.7 27.8 %copy-start.2 = (f32[128,128]{1,0:T(8,128)S(1)}, f32[128,128]{1,0:T(8,128)}, u32[]{:S(2)}) copy-start(f32[128,128]{1,0:T(8,128)} %first.1) | copy-start | bytes 196612
  60.8 28.0 %copy-start.4 = (f32[4,128]{1,0:T(4,128)S(1)}, f32[4,128]{1,0:T(4,128)}, u32[]{:S(2)}) copy-start(f32[4,128]{1,0:T(4,128)} %sensor.1) | copy-start | bytes 6148
  60.8 41.5 %copy-start = (bf16[128,16,256]{2,1,0:T(8,128)(2,1)S(1)}, bf16[128,16,256]{2,1,0:T(8,128)(2,1)}, u32[]{:S(2)}) copy-start(bf16[128,16,256]{2,1,0:T(8,128)(2,1)} %param.17) | copy-start | bytes 3145732
  61.5 3.5 %collective-permute-start = (bf16[4,256,128]{2,1,0:T(8,128)(2,1)S(1)}, bf16[4,256,128]{2,1,0:T(8,128)(2,1)S(1)}, u32[]{:S(2)}, u32[]{:S(2)}) collective-permute-start(bf16[4,256,128]{2,1,0:T(8,128)(2,1)S(1)} %get-tuple-element.23), channel_id=1, source_target_pairs={{0,1},{1,0},{2,3},{3,2},{4,5},{5,4},{6,7},{7,6},{8,9},{9,8},{10,11... | collective-permute-start | bytes 786440 | tf_op jit(solution)/shard_map/ppermute | solution.py:213
  65.1 10.1 %collective-permute-start.1 = (bf16[256,128]{1,0:T(8,128)(2,1)S(1)}, bf16[256,128]{1,0:T(8,128)(2,1)S(1)}, u32[]{:S(2)}, u32[]{:S(2)}) collective-permute-start(bf16[256,128]{1,0:T(8,128)(2,1)S(1)} %get-tuple-element.26), channel_id=1, source_target_pairs={{0,2},{2,4},{4,6},{6,0},{1,3},{3,5},{5,7},{7,1},{8,10},{10,12},{12... | collective-permute-start | bytes 196616 | tf_op jit(solution)/shard_map/ppermute | solution.py:216
  67.0 13.6 %collective-permute-start.3 = (bf16[256,128]{1,0:T(8,128)(2,1)S(1)}, bf16[256,128]{1,0:T(8,128)(2,1)S(1)}, u32[]{:S(2)}, u32[]{:S(2)}) collective-permute-start(bf16[256,128]{1,0:T(8,128)(2,1)S(1)} %get-tuple-element.27), channel_id=1, source_target_pairs={{0,6},{2,0},{4,2},{6,4},{1,7},{3,1},{5,3},{7,5},{8,14},{10,8},{12,... | collective-permute-start | bytes 196616 | tf_op jit(solution)/shard_map/ppermute | solution.py:217
  81.5 20.8 %all-to-all-start.3 = ((bf16[16,32,256]{2,1,0:T(8,128)(2,1)}), bf16[16,32,256]{2,1,0:T(8,128)(2,1)S(1)}, u32[]{:S(2)}, u32[]{:S(2)}) async-start(bf16[16,32,256]{2,1,0:T(8,128)(2,1)} %bitcast.12), calls=%async_computation.3 | async-start | bytes 524288 | tf_op jit(solution)/shard_map/all_to_all | solution.py:223
  89.0 32.2 %collective-permute-start.2 = (bf16[256,128]{1,0:T(8,128)(2,1)S(1)}, bf16[256,128]{1,0:T(8,128)(2,1)S(1)}, u32[]{:S(2)}, u32[]{:S(2)}) collective-permute-start(bf16[256,128]{1,0:T(8,128)(2,1)S(1)} %shard_map.124), channel_id=1, source_target_pairs={{0,2},{2,4},{4,6},{6,0},{1,3},{3,5},{5,7},{7,1},{8,10},{10,12},{12... | collective-permute-start | bytes 196616 | tf_op jit(solution)/shard_map/ppermute | solution.py:219
  103.8 17.4 %all-to-all-start.4 = ((f32[16,8,128]{2,1,0:T(8,128)}), f32[16,8,128]{2,1,0:T(8,128)S(1)}, u32[]{:S(2)}, u32[]{:S(2)}) async-start(f32[16,8,128]{2,1,0:T(8,128)} %shard_map.129), calls=%async_computation.4 | async-start | bytes 131072 | tf_op jit(solution)/shard_map/all_to_all | solution.py:238
  121.8 13.0 %all-to-all-start.5 = ((f32[8,8,128]{2,1,0:T(8,128)}), f32[8,8,128]{2,1,0:T(8,128)S(1)}, u32[]{:S(2)}, u32[]{:S(2)}) async-start(f32[8,8,128]{2,1,0:T(8,128)} %shard_map.130), calls=%async_computation.5 | async-start | bytes 65536 | tf_op jit(solution)/shard_map/all_to_all | solution.py:243

commit v5 on v4

--- a/solution.py
+++ b/solution.py
@@ -147,21 +147,25 @@
     prod = jnp.where(keep, prod, 0.0).reshape(HID, DS, n).sum(axis=1)
     pick = (iota((n // DS, n), 1) // DS == iota((n // DS, n), 0)).astype(F32)
     part = lax.dot_general(pick, prod, (((1,), (1,)), ((), ())), precision=HIGHEST, preferred_element_type=F32)
+    for to in range(L * C):
+        out[to] = part
+
+
+def spread_body(parts, out):
+    sums = []
+    for c in range(C):
+        total = parts[c]
+        for l in range(1, L):
+            total = total + parts[l * C + c]
+        sums.append(total)
+    total = jnp.concatenate(sums, axis=0)
     for to in range(X * Y):
-        out[to] = part
-
-
-def spread_body(parts, out):
+        out[to] = total
+
+
+def final_body(parts, slope, features, sensor_hot, first, sensor):
     total = parts[0]
     for i in range(1, X * Y):
-        total = total + parts[i]
-    for to in range(L * C):
-        out[to] = total
-
-
-def final_body(parts, slope, features, sensor_hot, first, sensor):
-    total = parts[0]
-    for i in range(1, L):
         total = total + parts[i]
     grad_pre = total * slope[...]
     across = (((0,), (0,)), ((), ()))
@@ -234,13 +238,12 @@
 
     (embed,) = call(join_body, [((rows, 128), BF)], [VMEM] * 3, shares[0], second, third, flops=2**18)
     bands = C * H * BD
-    (parts,) = call(hidden_grad_body, [((X * Y, bands // C, HID), F32)], [VMEM, VMEM], mine, weight, flops=2**28)
+    (parts,) = call(hidden_grad_body, [((L * C, bands // C, HID), F32)], [VMEM, VMEM], mine, weight, flops=2**28)
+    parts = lax.all_to_all(parts, ("l", "c"), 0, 0, tiled=True)
+    parts, *_ = lax.optimization_barrier((parts, second))
+    (parts,) = call(spread_body, [((X * Y, bands, HID), F32)], [VMEM], parts, flops=2**16)
     parts = lax.all_to_all(parts, ("x", "y"), 0, 0, tiled=True)
     (grad_out,) = call(out_grad_body, [((HID * DS, P2), F32)], [VMEM, VMEM], hidden_t, grads, flops=2**28)
-    parts, *_ = lax.optimization_barrier((parts, grad_out))
-    parts, *_ = lax.optimization_barrier((parts, second))
-    (parts,) = call(spread_body, [((L * C, bands // C, HID), F32)], [VMEM], parts, flops=2**16)
-    parts = lax.all_to_all(parts, ("l", "c"), 0, 0, tiled=True).reshape(L, bands, HID)
     grad_first, grad_sensor = call(
         final_body, [(first_weight.shape, F32), (sensor_embed.shape, F32)], [VMEM] * 4,
         parts, slope, features, sensor_hot, flops=2**20,

time: 137 us -> 135 us (0.985)
  blocking collectives: 37.6 us -> 31.8 us
  starting transfers between devices: 60.6 us -> 63.1 us
  waiting for transfers between devices: 19.9 us -> 22 us
    all_gather x1, blocking collectives: 8.41 us -> 2.59 us  [local(): grads = lax.all_gather(mine, 'c', axis=0, tiled=True)]
    all_to_all x1, starting transfers between devices: 8.07 us -> 10.5 us  [local(): parts = lax.all_to_all(parts, ('l', 'c'), 0, 0, tiled=True)]
    all_to_all x1, waiting for transfers between devices: 0.01 us -> 1.42 us  [local(): parts = lax.all_to_all(parts, ('x', 'y'), 0, 0, tiled=True)]
  transfers between devices with their start and end apart: 10 -> 10, of which waited for: 5 -> 6; matrix products, arithmetic and copies ran while one was open for 3% -> 3% of each run, Pallas kernels for 5% -> 5%
where the time goes in v5:
time: 135 us
  starting transfers between devices  63.1 us (47%)
  blocking collectives  31.8 us (24%)
  waiting for transfers between devices  22 us (16%)
  Pallas kernels  11.3 us (8%)
  other arithmetic  3.1 us (2%)
  local copies, waits for them, and re-layouts  1.78 us (1%)
    all_gather x1, blocking collectives, local(): lax.all_gather(cot_own, ('h', 'c'), axis=0, tiled=False)  29.2 us
    pallas_call x12, Pallas kernels, call(): pl.pallas_call(body, out_shape=[jax.ShapeDtypeStruct(shape, dtype) for sh...  11.3 us
    all_to_all x1, starting transfers between devices, local(): parts = lax.all_to_all(parts, ('l', 'c'), 0, 0, tiled=True)  10.5 us
    all_to_all x1, starting transfers between devices, local(): lax.all_to_all(grads.reshape(X * Y, L, BD * DS, P2), ('x', 'y'), 0, 0, ti...  7.35 us
    ppermute x1, starting transfers between devices, local(): third = lax.ppermute(shares[3], 'h', down)  7.27 us
    ppermute x1, starting transfers between devices, local(): second = lax.ppermute(second, 'h', up)  7.18 us
    all_to_all x1, starting transfers between devices, local(): parts = lax.all_to_all(parts, ('x', 'y'), 0, 0, tiled=True)  6.94 us
    all_to_all x1, starting transfers between devices, gather(): lax.all_to_all(jnp.broadcast_to(part[None], (count, *part.shape)), axes,...  6.75 us
  transfers between devices with their start and end apart: 10, of which 6 were waited for; matrix products, arithmetic and copies ran while one was open for 3% of the time, Pallas kernels for 5%

profile of v5, /device:TPU:1, one launch (start us, length us, event | category | flops | bytes accessed | tf_op | source)
XLA Modules:
  0.0 134.5 jit_solution(5460419973990813019)
XLA Ops:
  0.7 2.6 %shard_map.120 = bf16[4,32,256]{2,1,0:T(8,128)(2,1)} custom-call(s32[2]{0:T(128)} %idx.1, s32[2]{0:T(128)} %sens.1, f32[208]{0:T(256)} %table.1, f32[128,128]{1,0:T(8,128)} %first.1, f32[4,128]{1,0:T(4,128)} %sensor.1, bf16[2048,256]{1,0:T(8,128)(2,1)} %bitcast.41), custom_call_target="tpu_custom_call" | custom-call | flops 33554432 | bytes 1048576 | tf_op jit(solution)/shard_map/pallas_call | solution.py:26
  3.3 6.4 %all-to-all-start = ((bf16[4,32,256]{2,1,0:T(8,128)(2,1)}), bf16[4,32,256]{2,1,0:T(8,128)(2,1)S(1)}, u32[]{:S(2)}, u32[]{:S(2)}) async-start(bf16[4,32,256]{2,1,0:T(8,128)(2,1)} %shard_map.120), calls=%async_computation | async-start | bytes 131072 | tf_op jit(solution)/shard_map/all_to_all | solution.py:203
  11.3 3.0 %all-to-all-done = bf16[4,32,256]{2,1,0:T(8,128)(2,1)S(1)} async-done(((bf16[4,32,256]{2,1,0:T(8,128)(2,1)}), bf16[4,32,256]{2,1,0:T(8,128)(2,1)S(1)}, u32[]{:S(2)}, u32[]{:S(2)}) %all-to-all-start) | async-done | bytes 65568 | tf_op jit(solution)/shard_map/all_to_all | solution.py:203
  14.3 1.1 broadcast_in_dim.5
  15.4 6.8 %all-to-all-start.1 = ((bf16[16,128,256]{2,1,0:T(8,128)(2,1)}), bf16[16,128,256]{2,1,0:T(8,128)(2,1)S(1)}, u32[]{:S(2)}, u32[]{:S(2)}) async-start(bf16[16,128,256]{2,1,0:T(8,128)(2,1)} %broadcast_in_dim.5), calls=%async_computation.1 | async-start | bytes 2097152 | tf_op jit(solution)/shard_map/all_to_all | solution.py:186
  22.7 29.2 %all-gather = bf16[2176,128]{1,0:T(8,128)(2,1)S(1)} all-gather(bf16[272,128]{1,0:T(8,128)(2,1)S(1)} %pad_maximum_fusion), channel_id=2, replica_groups=mesh['x'=4,'y'=4,'l'=4,'h'=4,'c'=2] {'h','c'}, dimensions={0}, use_global_device_ids=true | all-gather | bytes 626688 | tf_op jit(solution)/shard_map/all_gather | solution.py:210
  51.9 1.5 %shard_map.121 = bf16[64,2,16,256]{3,2,1,0:T(8,128)(2,1)} custom-call(bf16[4,2,272,128]{3,2,1,0:T(8,128)(2,1)S(1)} %bitcast.45, bf16[256,512]{1,0:T(8,128)(2,1)S(1)} %bitcast.43), custom_call_target="tpu_custom_call" | custom-call | flops 268435456 | bytes 1048576 | tf_op jit(solution)/shard_map/pallas_call | solution.py:26
  53.4 7.4 %all-to-all-start.2 = ((bf16[16,4,32,256]{3,2,1,0:T(8,128)(2,1)}), bf16[16,4,32,256]{3,2,1,0:T(8,128)(2,1)S(1)}, u32[]{:S(2)}, u32[]{:S(2)}) async-start(bf16[16,4,32,256]{3,2,1,0:T(8,128)(2,1)} %bitcast.11), calls=%async_computation.2 | async-start | bytes 2097152 | tf_op jit(solution)/shard_map/all_to_all | solution.py:214
  61.5 2.4 %collective-permute-start = (bf16[4,256,128]{2,1,0:T(8,128)(2,1)S(1)}, bf16[4,256,128]{2,1,0:T(8,128)(2,1)S(1)}, u32[]{:S(2)}, u32[]{:S(2)}) collective-permute-start(bf16[4,256,128]{2,1,0:T(8,128)(2,1)S(1)} %get-tuple-element.22), channel_id=1, source_target_pairs={{0,1},{1,0},{2,3},{3,2},{4,5},{5,4},{6,7},{7,6},{8,9},{9,8},{10,11... | collective-permute-start | bytes 786440 | tf_op jit(solution)/shard_map/ppermute | solution.py:217
  63.9 1.1 collective-permute-done.other
  65.1 1.9 %collective-permute-start.1 = (bf16[256,128]{1,0:T(8,128)(2,1)S(1)}, bf16[256,128]{1,0:T(8,128)(2,1)S(1)}, u32[]{:S(2)}, u32[]{:S(2)}) collective-permute-start(bf16[256,128]{1,0:T(8,128)(2,1)S(1)} %get-tuple-element.25), channel_id=1, source_target_pairs={{0,2},{2,4},{4,6},{6,0},{1,3},{3,5},{5,7},{7,1},{8,10},{10,12},{12... | collective-permute-start | bytes 196616 | tf_op jit(solution)/shard_map/ppermute | solution.py:220
  67.0 7.3 %collective-permute-start.3 = (bf16[256,128]{1,0:T(8,128)(2,1)S(1)}, bf16[256,128]{1,0:T(8,128)(2,1)S(1)}, u32[]{:S(2)}, u32[]{:S(2)}) collective-permute-start(bf16[256,128]{1,0:T(8,128)(2,1)S(1)} %get-tuple-element.26), channel_id=1, source_target_pairs={{0,6},{2,0},{4,2},{6,4},{1,7},{3,1},{5,3},{7,5},{8,14},{10,8},{12,... | collective-permute-start | bytes 196616 | tf_op jit(solution)/shard_map/ppermute | solution.py:221
  75.2 5.4 %collective-permute-done.3.c = bf16[256,128]{1,0:T(8,128)(2,1)S(1)} collective-permute-done((bf16[256,128]{1,0:T(8,128)(2,1)S(1)}, bf16[256,128]{1,0:T(8,128)(2,1)S(1)}, u32[]{:S(2)}, u32[]{:S(2)}) %collective-permute-start.3) | collective-permute-done | bytes 65568 | tf_op jit(solution)/shard_map/ppermute | solution.py:221
  81.5 6.4 %all-to-all-start.3 = ((bf16[16,32,256]{2,1,0:T(8,128)(2,1)}), bf16[16,32,256]{2,1,0:T(8,128)(2,1)S(1)}, u32[]{:S(2)}, u32[]{:S(2)}) async-start(bf16[16,32,256]{2,1,0:T(8,128)(2,1)} %bitcast.12), calls=%async_computation.3 | async-start | bytes 524288 | tf_op jit(solution)/shard_map/all_to_all | solution.py:227
  89.0 7.2 %collective-permute-start.2 = (bf16[256,128]{1,0:T(8,128)(2,1)S(1)}, bf16[256,128]{1,0:T(8,128)(2,1)S(1)}, u32[]{:S(2)}, u32[]{:S(2)}) collective-permute-start(bf16[256,128]{1,0:T(8,128)(2,1)S(1)} %shard_map.124), channel_id=1, source_target_pairs={{0,2},{2,4},{4,6},{6,0},{1,3},{3,5},{5,7},{7,1},{8,10},{10,12},{12... | collective-permute-start | bytes 196616 | tf_op jit(solution)/shard_map/ppermute | solution.py:223
  96.2 6.1 %all-to-all-done.3 = bf16[16,32,256]{2,1,0:T(8,128)(2,1)S(1)} async-done(((bf16[16,32,256]{2,1,0:T(8,128)(2,1)}), bf16[16,32,256]{2,1,0:T(8,128)(2,1)S(1)}, u32[]{:S(2)}, u32[]{:S(2)}) %all-to-all-start.3) | async-done | bytes 262176 | tf_op jit(solution)/shard_map/all_to_all | solution.py:227
  102.3 1.4 %shard_map.129 = f32[8,8,128]{2,1,0:T(8,128)} custom-call(bf16[128,256]{1,0:T(8,128)(2,1)S(1)} %bitcast.48, bf16[2048,256]{1,0:T(8,128)(2,1)S(1)} %bitcast.42), custom_call_target="tpu_custom_call" | custom-call | flops 268435456 | bytes 1048576 | tf_op jit(solution)/shard_map/pallas_call | solution.py:26
  103.7 10.5 %all-to-all-start.4 = ((f32[8,8,128]{2,1,0:T(8,128)}), f32[8,8,128]{2,1,0:T(8,128)S(1)}, u32[]{:S(2)}, u32[]{:S(2)}) async-start(f32[8,8,128]{2,1,0:T(8,128)} %shard_map.129), calls=%async_computation.4 | async-start | bytes 65536 | tf_op jit(solution)/shard_map/all_to_all | solution.py:242
  114.3 4.9 %all-to-all-done.4.parts = f32[8,8,128]{2,1,0:T(8,128)S(1)} async-done(((f32[8,8,128]{2,1,0:T(8,128)}), f32[8,8,128]{2,1,0:T(8,128)S(1)}, u32[]{:S(2)}, u32[]{:S(2)}) %all-to-all-start.4) | async-done | bytes 32800 | tf_op jit(solution)/shard_map/all_to_all | solution.py:242
  119.9 6.9 %all-to-all-start.5 = ((f32[16,16,128]{2,1,0:T(8,128)}), f32[16,16,128]{2,1,0:T(8,128)S(1)}, u32[]{:S(2)}, u32[]{:S(2)}) async-start(f32[16,16,128]{2,1,0:T(8,128)} %shard_map.130), calls=%async_computation.5 | async-start | bytes 262144 | tf_op jit(solution)/shard_map/all_to_all | solution.py:245
  127.7 2.6 %all_gather.11.grads = bf16[256,256]{1,0:T(8,128)(2,1)S(1)} all-gather(bf16[128,256]{1,0:T(8,128)(2,1)S(1)} %bitcast.49), channel_id=1, replica_groups=mesh['x'=4,'y'=4,'l'=4,'h'=4,'c'=2] {'c'}, dimensions={0}, use_global_device_ids=true | all-gather | bytes 196608 | tf_op jit(solution)/shard_map/all_gather | solution.py:230
  130.3 1.9 %shard_map.128 = f32[2048,256]{1,0:T(8,128)} custom-call(bf16[128,16]{1,0:T(8,128)(2,1)S(1)} %copy.20.hidden_t, bf16[256,256]{1,0:T(8,128)(2,1)S(1)} %all_gather.11.grads), custom_call_target="tpu_custom_call" | custom-call | flops 268435456 | bytes 1048576 | tf_op jit(solution)/shard_map/pallas_call | solution.py:26
  132.2 1.4 %all-to-all-done.5.parts = f32[16,16,128]{2,1,0:T(8,128)S(1)} async-done(((f32[16,16,128]{2,1,0:T(8,128)}), f32[16,16,128]{2,1,0:T(8,128)S(1)}, u32[]{:S(2)}, u32[]{:S(2)}) %all-to-all-start.5) | async-done | bytes 131104 | tf_op jit(solution)/shard_map/all_to_all | solution.py:245
  133.6 0.9 shard_map.131
  (48 shorter events, 7.4 us)
Async XLA Ops:
  0.6 21.6 %copy-start.6 = (s32[16,2]{0,1:T(2,128)S(1)}, s32[16,2]{0,1:T(2,128)}, u32[]{:S(2)}) copy-start(s32[16,2]{0,1:T(2,128)} %param.11) | copy-start | bytes 388
  0.6 21.7 %copy-start.3 = (bf16[256,2,256]{2,1,0:T(2,128)(2,1)S(1)}, bf16[256,2,256]{2,1,0:T(2,128)(2,1)}, u32[]{:S(2)}) copy-start(bf16[256,2,256]{2,1,0:T(2,128)(2,1)} %param.9) | copy-start | bytes 786436
  3.3 11.0 %all-to-all-start = ((bf16[4,32,256]{2,1,0:T(8,128)(2,1)}), bf16[4,32,256]{2,1,0:T(8,128)(2,1)S(1)}, u32[]{:S(2)}, u32[]{:S(2)}) async-start(bf16[4,32,256]{2,1,0:T(8,128)(2,1)} %shard_map.120), calls=%async_computation | async-start | bytes 131072 | tf_op jit(solution)/shard_map/all_to_all | solution.py:203
  15.4 38.0 %all-to-all-start.1 = ((bf16[16,128,256]{2,1,0:T(8,128)(2,1)}), bf16[16,128,256]{2,1,0:T(8,128)(2,1)S(1)}, u32[]{:S(2)}, u32[]{:S(2)}) async-start(bf16[16,128,256]{2,1,0:T(8,128)(2,1)} %broadcast_in_dim.5), calls=%async_computation.1 | async-start | bytes 2097152 | tf_op jit(solution)/shard_map/all_to_all | solution.py:186
  51.9 1.5 %copy-start.1 = (bf16[2176,128]{1,0:T(8,128)(2,1)}, bf16[2176,128]{1,0:T(8,128)(2,1)S(1)}, u32[]{:S(2)}) copy-start(bf16[2176,128]{1,0:T(8,128)(2,1)S(1)} %all-gather) | copy-start | bytes 1671172
  53.4 27.2 %all-to-all-start.2 = ((bf16[16,4,32,256]{3,2,1,0:T(8,128)(2,1)}), bf16[16,4,32,256]{3,2,1,0:T(8,128)(2,1)S(1)}, u32[]{:S(2)}, u32[]{:S(2)}) async-start(bf16[16,4,32,256]{3,2,1,0:T(8,128)(2,1)} %bitcast.11), calls=%async_computation.2 | async-start | bytes 2097152 | tf_op jit(solution)/shard_map/all_to_all | solution.py:214
  60.7 27.4 %copy-start.5 = (f32[208]{0:T(256)S(1)}, f32[208]{0:T(256)}, u32[]{:S(2)}) copy-start(f32[208]{0:T(256)} %table.1) | copy-start | bytes 2500
  60.7 27.8 %copy-start.2 = (f32[128,128]{1,0:T(8,128)S(1)}, f32[128,128]{1,0:T(8,128)}, u32[]{:S(2)}) copy-start(f32[128,128]{1,0:T(8,128)} %first.1) | copy-start | bytes 196612
  60.8 28.0 %copy-start.4 = (f32[4,128]{1,0:T(4,128)S(1)}, f32[4,128]{1,0:T(4,128)}, u32[]{:S(2)}) copy-start(f32[4,128]{1,0:T(4,128)} %sensor.1) | copy-start | bytes 6148
  60.8 41.5 %copy-start = (bf16[128,16,256]{2,1,0:T(8,128)(2,1)S(1)}, bf16[128,16,256]{2,1,0:T(8,128)(2,1)}, u32[]{:S(2)}) copy-start(bf16[128,16,256]{2,1,0:T(8,128)(2,1)} %param.17) | copy-start | bytes 3145732
  61.5 3.5 %collective-permute-start = (bf16[4,256,128]{2,1,0:T(8,128)(2,1)S(1)}, bf16[4,256,128]{2,1,0:T(8,128)(2,1)S(1)}, u32[]{:S(2)}, u32[]{:S(2)}) collective-permute-start(bf16[4,256,128]{2,1,0:T(8,128)(2,1)S(1)} %get-tuple-element.22), channel_id=1, source_target_pairs={{0,1},{1,0},{2,3},{3,2},{4,5},{5,4},{6,7},{7,6},{8,9},{9,8},{10,11... | collective-permute-start | bytes 786440 | tf_op jit(solution)/shard_map/ppermute | solution.py:217
  65.1 10.1 %collective-permute-start.1 = (bf16[256,128]{1,0:T(8,128)(2,1)S(1)}, bf16[256,128]{1,0:T(8,128)(2,1)S(1)}, u32[]{:S(2)}, u32[]{:S(2)}) collective-permute-start(bf16[256,128]{1,0:T(8,128)(2,1)S(1)} %get-tuple-element.25), channel_id=1, source_target_pairs={{0,2},{2,4},{4,6},{6,0},{1,3},{3,5},{5,7},{7,1},{8,10},{10,12},{12... | collective-permute-start | bytes 196616 | tf_op jit(solution)/shard_map/ppermute | solution.py:220
  67.0 13.6 %collective-permute-start.3 = (bf16[256,128]{1,0:T(8,128)(2,1)S(1)}, bf16[256,128]{1,0:T(8,128)(2,1)S(1)}, u32[]{:S(2)}, u32[]{:S(2)}) collective-permute-start(bf16[256,128]{1,0:T(8,128)(2,1)S(1)} %get-tuple-element.26), channel_id=1, source_target_pairs={{0,6},{2,0},{4,2},{6,4},{1,7},{3,1},{5,3},{7,5},{8,14},{10,8},{12,... | collective-permute-start | bytes 196616 | tf_op jit(solution)/shard_map/ppermute | solution.py:221
  81.5 20.8 %all-to-all-start.3 = ((bf16[16,32,256]{2,1,0:T(8,128)(2,1)}), bf16[16,32,256]{2,1,0:T(8,128)(2,1)S(1)}, u32[]{:S(2)}, u32[]{:S(2)}) async-start(bf16[16,32,256]{2,1,0:T(8,128)(2,1)} %bitcast.12), calls=%async_computation.3 | async-start | bytes 524288 | tf_op jit(solution)/shard_map/all_to_all | solution.py:227
  89.0 25.3 %collective-permute-start.2 = (bf16[256,128]{1,0:T(8,128)(2,1)S(1)}, bf16[256,128]{1,0:T(8,128)(2,1)S(1)}, u32[]{:S(2)}, u32[]{:S(2)}) collective-permute-start(bf16[256,128]{1,0:T(8,128)(2,1)S(1)} %shard_map.124), channel_id=1, source_target_pairs={{0,2},{2,4},{4,6},{6,0},{1,3},{3,5},{5,7},{7,1},{8,10},{10,12},{12... | collective-permute-start | bytes 196616 | tf_op jit(solution)/shard_map/ppermute | solution.py:223
  103.7 15.5 %all-to-all-start.4 = ((f32[8,8,128]{2,1,0:T(8,128)}), f32[8,8,128]{2,1,0:T(8,128)S(1)}, u32[]{:S(2)}, u32[]{:S(2)}) async-start(f32[8,8,128]{2,1,0:T(8,128)} %shard_map.129), calls=%async_computation.4 | async-start | bytes 65536 | tf_op jit(solution)/shard_map/all_to_all | solution.py:242
  119.9 13.7 %all-to-all-start.5 = ((f32[16,16,128]{2,1,0:T(8,128)}), f32[16,16,128]{2,1,0:T(8,128)S(1)}, u32[]{:S(2)}, u32[]{:S(2)}) async-start(f32[16,16,128]{2,1,0:T(8,128)} %shard_map.130), calls=%async_computation.5 | async-start | bytes 262144 | tf_op jit(solution)/shard_map/all_to_all | solution.py:245

commit v6 on v5

--- a/solution.py
+++ b/solution.py
@@ -222,9 +222,10 @@
     (second,) = call(add_body, [((rows, 128), BF)], [VMEM] * 2, shares[1], first, flops=2**16)
     second = lax.ppermute(second, "h", up)
 
-    grads, *_ = lax.optimization_barrier((grads, first, third))
+    grads, *_ = lax.optimization_barrier((grads, first))
     (grads,) = call(sum_xy_body, [((L, H, BD * DS, P2), BF)], [VMEM], grads, flops=2**20)
     grads = lax.all_to_all(grads.reshape(L * H, BD * DS, P2), ("l", "h"), 0, 0, tiled=True)
+    grads, *_ = lax.optimization_barrier((grads, third))
     (grads,) = call(sum_l_body, [((H, BD * DS, P2), BF)], [VMEM], grads.reshape(L, H, BD * DS, P2), flops=2**18)
     mine = grads.reshape(H * BD * DS, P2)
     grads = lax.all_gather(mine, "c", axis=0, tiled=True)
@@ -240,10 +241,10 @@
     bands = C * H * BD
     (parts,) = call(hidden_grad_body, [((L * C, bands // C, HID), F32)], [VMEM, VMEM], mine, weight, flops=2**28)
     parts = lax.all_to_all(parts, ("l", "c"), 0, 0, tiled=True)
-    parts, *_ = lax.optimization_barrier((parts, second))
+    (grad_out,) = call(out_grad_body, [((HID * DS, P2), F32)], [VMEM, VMEM], hidden_t, grads, flops=2**28)
+    parts, *_ = lax.optimization_barrier((parts, second, grad_out))
     (parts,) = call(spread_body, [((X * Y, bands, HID), F32)], [VMEM], parts, flops=2**16)
     parts = lax.all_to_all(parts, ("x", "y"), 0, 0, tiled=True)
-    (grad_out,) = call(out_grad_body, [((HID * DS, P2), F32)], [VMEM, VMEM], hidden_t, grads, flops=2**28)
     grad_first, grad_sensor = call(
         final_body, [(first_weight.shape, F32), (sensor_embed.shape, F32)], [VMEM] * 4,
         parts, slope, features, sensor_hot, flops=2**20,

time: 135 us -> 136 us (level)
  waiting for transfers between devices: 22 us -> 25.1 us
  starting transfers between devices: 63.1 us -> 61.1 us
    ppermute x1, waiting for transfers between devices: 0.01 us -> 6.18 us  [local(): first = lax.ppermute(shares[2], 'h', up)]
    all_to_all x1, waiting for transfers between devices: 6.1 us -> 0.01 us  [local(): lax.all_to_all(grads.reshape(L * H, BD * DS, P2), ('l', 'h'), 0, 0, tiled...]
    ppermute x1, starting transfers between devices: 7.18 us -> 2.01 us  [local(): second = lax.ppermute(second, 'h', up)]
    all_to_all x1, waiting for transfers between devices: 1.42 us -> 6.01 us  [local(): parts = lax.all_to_all(parts, ('x', 'y'), 0, 0, tiled=True)]
    all_to_all x1, waiting for transfers between devices: 4.94 us -> 1.06 us  [local(): parts = lax.all_to_all(parts, ('l', 'c'), 0, 0, tiled=True)]
    all_to_all x1, waiting for transfers between devices: 0.01 us -> 2.7 us  [local(): lax.all_to_all(grads.reshape(X * Y, L, BD * DS, P2), ('x', 'y'), 0, 0, ti...]
    all_to_all x1, starting transfers between devices: 10.5 us -> 12.6 us  [local(): parts = lax.all_to_all(parts, ('l', 'c'), 0, 0, tiled=True)]
  transfers between devices with their start and end apart: 10 -> 10, of which waited for: 6 -> 7; matrix products, arithmetic and copies ran while one was open for 3% -> 3% of each run, Pallas kernels for 5% -> 5%
where the time goes in v6:
time: 136 us; the launch traced here: 135 us
  starting transfers between devices  61.1 us (45%)
  blocking collectives  31.1 us (23%)
  waiting for transfers between devices  25.1 us (18%)
  Pallas kernels  11.3 us (8%)
  other arithmetic  3.1 us (2%)
  local copies, waits for them, and re-layouts  1.78 us (1%)
    all_gather x1, blocking collectives, local(): lax.all_gather(cot_own, ('h', 'c'), axis=0, tiled=False)  29.2 us
    all_to_all x1, starting transfers between devices, local(): parts = lax.all_to_all(parts, ('l', 'c'), 0, 0, tiled=True)  12.6 us
    pallas_call x12, Pallas kernels, call(): pl.pallas_call(body, out_shape=[jax.ShapeDtypeStruct(shape, dtype) for sh...  11.3 us
    all_to_all x1, starting transfers between devices, local(): parts = lax.all_to_all(parts, ('x', 'y'), 0, 0, tiled=True)  8.01 us
    all_to_all x1, starting transfers between devices, local(): lax.all_to_all(grads.reshape(X * Y, L, BD * DS, P2), ('x', 'y'), 0, 0, ti...  7.35 us
    ppermute x1, starting transfers between devices, local(): third = lax.ppermute(shares[3], 'h', down)  7.19 us
    all_to_all x1, starting transfers between devices, gather(): lax.all_to_all(jnp.broadcast_to(part[None], (count, *part.shape)), axes,...  6.75 us
    all_to_all x1, starting transfers between devices, local(): lax.all_to_all(grads.reshape(L * H, BD * DS, P2), ('l', 'h'), 0, 0, tiled...  6.47 us
  transfers between devices with their start and end apart: 10, of which 7 were waited for; matrix products, arithmetic and copies ran while one was open for 3% of the time, Pallas kernels for 5%

profile of v6, /device:TPU:1, one launch (start us, length us, event | category | flops | bytes accessed | tf_op | source)
XLA Modules:
  0.0 134.9 jit_solution(13933040203471666254)
XLA Ops:
  0.7 2.6 %shard_map.120 = bf16[4,32,256]{2,1,0:T(8,128)(2,1)} custom-call(s32[2]{0:T(128)} %idx.1, s32[2]{0:T(128)} %sens.1, f32[208]{0:T(256)} %table.1, f32[128,128]{1,0:T(8,128)} %first.1, f32[4,128]{1,0:T(4,128)} %sensor.1, bf16[2048,256]{1,0:T(8,128)(2,1)} %bitcast.41), custom_call_target="tpu_custom_call" | custom-call | flops 33554432 | bytes 1048576 | tf_op jit(solution)/shard_map/pallas_call | solution.py:26
  3.3 6.4 %all-to-all-start = ((bf16[4,32,256]{2,1,0:T(8,128)(2,1)}), bf16[4,32,256]{2,1,0:T(8,128)(2,1)S(1)}, u32[]{:S(2)}, u32[]{:S(2)}) async-start(bf16[4,32,256]{2,1,0:T(8,128)(2,1)} %shard_map.120), calls=%async_computation | async-start | bytes 131072 | tf_op jit(solution)/shard_map/all_to_all | solution.py:203
  11.3 3.0 %all-to-all-done = bf16[4,32,256]{2,1,0:T(8,128)(2,1)S(1)} async-done(((bf16[4,32,256]{2,1,0:T(8,128)(2,1)}), bf16[4,32,256]{2,1,0:T(8,128)(2,1)S(1)}, u32[]{:S(2)}, u32[]{:S(2)}) %all-to-all-start) | async-done | bytes 65568 | tf_op jit(solution)/shard_map/all_to_all | solution.py:203
  14.3 1.1 broadcast_in_dim.5
  15.4 6.8 %all-to-all-start.1 = ((bf16[16,128,256]{2,1,0:T(8,128)(2,1)}), bf16[16,128,256]{2,1,0:T(8,128)(2,1)S(1)}, u32[]{:S(2)}, u32[]{:S(2)}) async-start(bf16[16,128,256]{2,1,0:T(8,128)(2,1)} %broadcast_in_dim.5), calls=%async_computation.1 | async-start | bytes 2097152 | tf_op jit(solution)/shard_map/all_to_all | solution.py:186
  22.7 29.2 %all-gather = bf16[2176,128]{1,0:T(8,128)(2,1)S(1)} all-gather(bf16[272,128]{1,0:T(8,128)(2,1)S(1)} %pad_maximum_fusion), channel_id=2, replica_groups=mesh['x'=4,'y'=4,'l'=4,'h'=4,'c'=2] {'h','c'}, dimensions={0}, use_global_device_ids=true | all-gather | bytes 626688 | tf_op jit(solution)/shard_map/all_gather | solution.py:210
  51.9 1.5 %shard_map.121 = bf16[64,2,16,256]{3,2,1,0:T(8,128)(2,1)} custom-call(bf16[4,2,272,128]{3,2,1,0:T(8,128)(2,1)S(1)} %bitcast.45, bf16[256,512]{1,0:T(8,128)(2,1)S(1)} %bitcast.43), custom_call_target="tpu_custom_call" | custom-call | flops 268435456 | bytes 1048576 | tf_op jit(solution)/shard_map/pallas_call | solution.py:26
  53.4 7.4 %all-to-all-start.2 = ((bf16[16,4,32,256]{3,2,1,0:T(8,128)(2,1)}), bf16[16,4,32,256]{3,2,1,0:T(8,128)(2,1)S(1)}, u32[]{:S(2)}, u32[]{:S(2)}) async-start(bf16[16,4,32,256]{3,2,1,0:T(8,128)(2,1)} %bitcast.11), calls=%async_computation.2 | async-start | bytes 2097152 | tf_op jit(solution)/shard_map/all_to_all | solution.py:214
  61.5 2.4 %collective-permute-start = (bf16[4,256,128]{2,1,0:T(8,128)(2,1)S(1)}, bf16[4,256,128]{2,1,0:T(8,128)(2,1)S(1)}, u32[]{:S(2)}, u32[]{:S(2)}) collective-permute-start(bf16[4,256,128]{2,1,0:T(8,128)(2,1)S(1)} %get-tuple-element.23), channel_id=1, source_target_pairs={{0,1},{1,0},{2,3},{3,2},{4,5},{5,4},{6,7},{7,6},{8,9},{9,8},{10,11... | collective-permute-start | bytes 786440 | tf_op jit(solution)/shard_map/ppermute | solution.py:217
  63.9 1.1 collective-permute-done.other
  65.1 1.9 %collective-permute-start.1 = (bf16[256,128]{1,0:T(8,128)(2,1)S(1)}, bf16[256,128]{1,0:T(8,128)(2,1)S(1)}, u32[]{:S(2)}, u32[]{:S(2)}) collective-permute-start(bf16[256,128]{1,0:T(8,128)(2,1)S(1)} %get-tuple-element.26), channel_id=1, source_target_pairs={{0,2},{2,4},{4,6},{6,0},{1,3},{3,5},{5,7},{7,1},{8,10},{10,12},{12... | collective-permute-start | bytes 196616 | tf_op jit(solution)/shard_map/ppermute | solution.py:220
  67.9 6.2 %collective-permute-done.1.b = bf16[256,128]{1,0:T(8,128)(2,1)S(1)} collective-permute-done((bf16[256,128]{1,0:T(8,128)(2,1)S(1)}, bf16[256,128]{1,0:T(8,128)(2,1)S(1)}, u32[]{:S(2)}, u32[]{:S(2)}) %collective-permute-start.1) | collective-permute-done | bytes 65568 | tf_op jit(solution)/shard_map/ppermute | solution.py:220
  74.1 2.7 %all-to-all-done.2.parts = bf16[16,4,32,256]{3,2,1,0:T(8,128)(2,1)S(1)} async-done(((bf16[16,4,32,256]{3,2,1,0:T(8,128)(2,1)}), bf16[16,4,32,256]{3,2,1,0:T(8,128)(2,1)S(1)}, u32[]{:S(2)}, u32[]{:S(2)}) %all-to-all-start.2) | async-done | bytes 1048608 | tf_op jit(solution)/shard_map/all_to_all | solution.py:214
  77.6 6.5 %all-to-all-start.3 = ((bf16[16,32,256]{2,1,0:T(8,128)(2,1)}), bf16[16,32,256]{2,1,0:T(8,128)(2,1)S(1)}, u32[]{:S(2)}, u32[]{:S(2)}) async-start(bf16[16,32,256]{2,1,0:T(8,128)(2,1)} %bitcast.12), calls=%async_computation.3 | async-start | bytes 524288 | tf_op jit(solution)/shard_map/all_to_all | solution.py:227
  85.0 7.2 %collective-permute-start.3 = (bf16[256,128]{1,0:T(8,128)(2,1)S(1)}, bf16[256,128]{1,0:T(8,128)(2,1)S(1)}, u32[]{:S(2)}, u32[]{:S(2)}) collective-permute-start(bf16[256,128]{1,0:T(8,128)(2,1)S(1)} %get-tuple-element.27), channel_id=1, source_target_pairs={{0,6},{2,0},{4,2},{6,4},{1,7},{3,1},{5,3},{7,5},{8,14},{10,8},{12,... | collective-permute-start | bytes 196616 | tf_op jit(solution)/shard_map/ppermute | solution.py:221
  92.5 2.0 %collective-permute-start.2 = (bf16[256,128]{1,0:T(8,128)(2,1)S(1)}, bf16[256,128]{1,0:T(8,128)(2,1)S(1)}, u32[]{:S(2)}, u32[]{:S(2)}) collective-permute-start(bf16[256,128]{1,0:T(8,128)(2,1)S(1)} %shard_map.124), channel_id=1, source_target_pairs={{0,2},{2,4},{4,6},{6,0},{1,3},{3,5},{5,7},{7,1},{8,10},{10,12},{12... | collective-permute-start | bytes 196616 | tf_op jit(solution)/shard_map/ppermute | solution.py:223
  94.5 5.1 %collective-permute-done.3.c = bf16[256,128]{1,0:T(8,128)(2,1)S(1)} collective-permute-done((bf16[256,128]{1,0:T(8,128)(2,1)S(1)}, bf16[256,128]{1,0:T(8,128)(2,1)S(1)}, u32[]{:S(2)}, u32[]{:S(2)}) %collective-permute-start.3) | collective-permute-done | bytes 65568 | tf_op jit(solution)/shard_map/ppermute | solution.py:221
  99.6 1.4 %shard_map.129 = f32[8,8,128]{2,1,0:T(8,128)} custom-call(bf16[128,256]{1,0:T(8,128)(2,1)S(1)} %bitcast.48, bf16[2048,256]{1,0:T(8,128)(2,1)S(1)} %bitcast.42), custom_call_target="tpu_custom_call" | custom-call | flops 268435456 | bytes 1048576 | tf_op jit(solution)/shard_map/pallas_call | solution.py:26
  101.0 12.6 %all-to-all-start.4 = ((f32[8,8,128]{2,1,0:T(8,128)}), f32[8,8,128]{2,1,0:T(8,128)S(1)}, u32[]{:S(2)}, u32[]{:S(2)}) async-start(f32[8,8,128]{2,1,0:T(8,128)} %shard_map.129), calls=%async_computation.4 | async-start | bytes 65536 | tf_op jit(solution)/shard_map/all_to_all | solution.py:243
  113.8 1.9 %all_gather.11.grads = bf16[256,256]{1,0:T(8,128)(2,1)S(1)} all-gather(bf16[128,256]{1,0:T(8,128)(2,1)S(1)} %bitcast.49), channel_id=1, replica_groups=mesh['x'=4,'y'=4,'l'=4,'h'=4,'c'=2] {'c'}, dimensions={0}, use_global_device_ids=true | all-gather | bytes 196608 | tf_op jit(solution)/shard_map/all_gather | solution.py:231
  115.7 1.9 %shard_map.128 = f32[2048,256]{1,0:T(8,128)} custom-call(bf16[128,16]{1,0:T(8,128)(2,1)S(1)} %copy.20.hidden_t, bf16[256,256]{1,0:T(8,128)(2,1)S(1)} %all_gather.11.grads), custom_call_target="tpu_custom_call" | custom-call | flops 268435456 | bytes 1048576 | tf_op jit(solution)/shard_map/pallas_call | solution.py:26
  117.6 1.1 all-to-all-done.4.parts
  119.3 8.0 %all-to-all-start.5 = ((f32[16,16,128]{2,1,0:T(8,128)}), f32[16,16,128]{2,1,0:T(8,128)S(1)}, u32[]{:S(2)}, u32[]{:S(2)}) async-start(f32[16,16,128]{2,1,0:T(8,128)} %shard_map.130), calls=%async_computation.5 | async-start | bytes 262144 | tf_op jit(solution)/shard_map/all_to_all | solution.py:247
  128.0 6.0 %all-to-all-done.5.parts = f32[16,16,128]{2,1,0:T(8,128)S(1)} async-done(((f32[16,16,128]{2,1,0:T(8,128)}), f32[16,16,128]{2,1,0:T(8,128)S(1)}, u32[]{:S(2)}, u32[]{:S(2)}) %all-to-all-start.5) | async-done | bytes 131104 | tf_op jit(solution)/shard_map/all_to_all | solution.py:247
  (48 shorter events, 8.2 us)
Async XLA Ops:
  0.6 21.6 %copy-start.6 = (s32[16,2]{0,1:T(2,128)S(1)}, s32[16,2]{0,1:T(2,128)}, u32[]{:S(2)}) copy-start(s32[16,2]{0,1:T(2,128)} %param.11) | copy-start | bytes 388
  0.6 21.7 %copy-start.3 = (bf16[256,2,256]{2,1,0:T(2,128)(2,1)S(1)}, bf16[256,2,256]{2,1,0:T(2,128)(2,1)}, u32[]{:S(2)}) copy-start(bf16[256,2,256]{2,1,0:T(2,128)(2,1)} %param.9) | copy-start | bytes 786436
  3.3 11.0 %all-to-all-start = ((bf16[4,32,256]{2,1,0:T(8,128)(2,1)}), bf16[4,32,256]{2,1,0:T(8,128)(2,1)S(1)}, u32[]{:S(2)}, u32[]{:S(2)}) async-start(bf16[4,32,256]{2,1,0:T(8,128)(2,1)} %shard_map.120), calls=%async_computation | async-start | bytes 131072 | tf_op jit(solution)/shard_map/all_to_all | solution.py:203
  15.4 38.0 %all-to-all-start.1 = ((bf16[16,128,256]{2,1,0:T(8,128)(2,1)}), bf16[16,128,256]{2,1,0:T(8,128)(2,1)S(1)}, u32[]{:S(2)}, u32[]{:S(2)}) async-start(bf16[16,128,256]{2,1,0:T(8,128)(2,1)} %broadcast_in_dim.5), calls=%async_computation.1 | async-start | bytes 2097152 | tf_op jit(solution)/shard_map/all_to_all | solution.py:186
  51.9 1.5 %copy-start.1 = (bf16[2176,128]{1,0:T(8,128)(2,1)}, bf16[2176,128]{1,0:T(8,128)(2,1)S(1)}, u32[]{:S(2)}) copy-start(bf16[2176,128]{1,0:T(8,128)(2,1)S(1)} %all-gather) | copy-start | bytes 1671172
  53.4 23.4 %all-to-all-start.2 = ((bf16[16,4,32,256]{3,2,1,0:T(8,128)(2,1)}), bf16[16,4,32,256]{3,2,1,0:T(8,128)(2,1)S(1)}, u32[]{:S(2)}, u32[]{:S(2)}) async-start(bf16[16,4,32,256]{3,2,1,0:T(8,128)(2,1)} %bitcast.11), calls=%async_computation.2 | async-start | bytes 2097152 | tf_op jit(solution)/shard_map/all_to_all | solution.py:214
  60.7 23.7 %copy-start.5 = (f32[208]{0:T(256)S(1)}, f32[208]{0:T(256)}, u32[]{:S(2)}) copy-start(f32[208]{0:T(256)} %table.1) | copy-start | bytes 2500
  60.7 24.1 %copy-start.2 = (f32[128,128]{1,0:T(8,128)S(1)}, f32[128,128]{1,0:T(8,128)}, u32[]{:S(2)}) copy-start(f32[128,128]{1,0:T(8,128)} %first.1) | copy-start | bytes 196612
  60.8 31.5 %copy-start.4 = (f32[4,128]{1,0:T(4,128)S(1)}, f32[4,128]{1,0:T(4,128)}, u32[]{:S(2)}) copy-start(f32[4,128]{1,0:T(4,128)} %sensor.1) | copy-start | bytes 6148
  60.8 38.8 %copy-start = (bf16[128,16,256]{2,1,0:T(8,128)(2,1)S(1)}, bf16[128,16,256]{2,1,0:T(8,128)(2,1)}, u32[]{:S(2)}) copy-start(bf16[128,16,256]{2,1,0:T(8,128)(2,1)} %param.17) | copy-start | bytes 3145732
  61.5 3.5 %collective-permute-start = (bf16[4,256,128]{2,1,0:T(8,128)(2,1)S(1)}, bf16[4,256,128]{2,1,0:T(8,128)(2,1)S(1)}, u32[]{:S(2)}, u32[]{:S(2)}) collective-permute-start(bf16[4,256,128]{2,1,0:T(8,128)(2,1)S(1)} %get-tuple-element.23), channel_id=1, source_target_pairs={{0,1},{1,0},{2,3},{3,2},{4,5},{5,4},{6,7},{7,6},{8,9},{9,8},{10,11... | collective-permute-start | bytes 786440 | tf_op jit(solution)/shard_map/ppermute | solution.py:217
  65.1 9.0 %collective-permute-start.1 = (bf16[256,128]{1,0:T(8,128)(2,1)S(1)}, bf16[256,128]{1,0:T(8,128)(2,1)S(1)}, u32[]{:S(2)}, u32[]{:S(2)}) collective-permute-start(bf16[256,128]{1,0:T(8,128)(2,1)S(1)} %get-tuple-element.26), channel_id=1, source_target_pairs={{0,2},{2,4},{4,6},{6,0},{1,3},{3,5},{5,7},{7,1},{8,10},{10,12},{12... | collective-permute-start | bytes 196616 | tf_op jit(solution)/shard_map/ppermute | solution.py:220
  77.6 21.9 %all-to-all-start.3 = ((bf16[16,32,256]{2,1,0:T(8,128)(2,1)}), bf16[16,32,256]{2,1,0:T(8,128)(2,1)S(1)}, u32[]{:S(2)}, u32[]{:S(2)}) async-start(bf16[16,32,256]{2,1,0:T(8,128)(2,1)} %bitcast.12), calls=%async_computation.3 | async-start | bytes 524288 | tf_op jit(solution)/shard_map/all_to_all | solution.py:227
  85.0 14.5 %collective-permute-start.3 = (bf16[256,128]{1,0:T(8,128)(2,1)S(1)}, bf16[256,128]{1,0:T(8,128)(2,1)S(1)}, u32[]{:S(2)}, u32[]{:S(2)}) collective-permute-start(bf16[256,128]{1,0:T(8,128)(2,1)S(1)} %get-tuple-element.27), channel_id=1, source_target_pairs={{0,6},{2,0},{4,2},{6,4},{1,7},{3,1},{5,3},{7,5},{8,14},{10,8},{12,... | collective-permute-start | bytes 196616 | tf_op jit(solution)/shard_map/ppermute | solution.py:221
  92.5 25.1 %collective-permute-start.2 = (bf16[256,128]{1,0:T(8,128)(2,1)S(1)}, bf16[256,128]{1,0:T(8,128)(2,1)S(1)}, u32[]{:S(2)}, u32[]{:S(2)}) collective-permute-start(bf16[256,128]{1,0:T(8,128)(2,1)S(1)} %shard_map.124), channel_id=1, source_target_pairs={{0,2},{2,4},{4,6},{6,0},{1,3},{3,5},{5,7},{7,1},{8,10},{10,12},{12... | collective-permute-start | bytes 196616 | tf_op jit(solution)/shard_map/ppermute | solution.py:223
  101.0 17.6 %all-to-all-start.4 = ((f32[8,8,128]{2,1,0:T(8,128)}), f32[8,8,128]{2,1,0:T(8,128)S(1)}, u32[]{:S(2)}, u32[]{:S(2)}) async-start(f32[8,8,128]{2,1,0:T(8,128)} %shard_map.129), calls=%async_computation.4 | async-start | bytes 65536 | tf_op jit(solution)/shard_map/all_to_all | solution.py:243
  119.3 14.8 %all-to-all-start.5 = ((f32[16,16,128]{2,1,0:T(8,128)}), f32[16,16,128]{2,1,0:T(8,128)S(1)}, u32[]{:S(2)}, u32[]{:S(2)}) async-start(f32[16,16,128]{2,1,0:T(8,128)} %shard_map.130), calls=%async_computation.5 | async-start | bytes 262144 | tf_op jit(solution)/shard_map/all_to_all | solution.py:247
